TPU v7x, 512 devices: a whole 4x4x16 slice. The times are simulated.
512 devices in a mesh: gx: 32 (over y, x, core), gy: 16 (over z).
Axes of the slice: x: 4, y: 4, z: 16, core: 2. Of those that a mesh axis runs over, the one named last changes fastest.
Arguments:
- basis: float32 [32, 256, 128, 256], P(None, 'gx', 'gy'), may hold values from -6 to 6
- rhs: float32 [256, 128, 256], P('gx', 'gy'), may hold values from -12 to 12
- extra_diag: float32 [256, 128, 256], P('gx', 'gy'), may hold values from 0.02 to 0.5
- coeff: float32 [3, 256, 128, 256], P(None, 'gx', 'gy'), may hold values from 0.3 to 3
Outputs:
- guess: float32 [256, 128, 256], P('gx', 'gy')
- stepped: float32 [256, 128, 256], P('gx', 'gy')
All inputs are finite; a program needn't handle non-finite values.
Results may differ from a plain program's by a relative error of at most 0.0003.
Values sent between devices are 32-bit elements; how exact they have to be, the bound alone decides.
A program may use at most 64 MiB of HBM per device.

v0:
```python
import jax
import jax.numpy as jnp
from jax import lax
from jax.sharding import PartitionSpec as P

precise = lax.Precision.HIGHEST


def shifted(block, axis, distance):
    devices = range(lax.axis_size(axis))
    route = [(i - distance, i) for i in devices if i - distance in devices]
    return lax.ppermute(block, axis, route)


def padded_2(cells, sides, width):
    for axis, dim in sides:
        count = lax.axis_size(axis)
        ends = count - 1
        head = lax.slice_in_dim(cells, 0, width, axis=dim)
        tail = lax.slice_in_dim(cells, cells.shape[dim] - width, cells.shape[dim], axis=dim)
        cells = jnp.concatenate(
            [
                lax.ppermute(tail, axis, [(i, (i + 1) % count) for i in range(ends)]),
                cells,
                lax.ppermute(head, axis, [((i + 1) % count, i) for i in range(ends)]),
            ],
            axis=dim,
        )
    return cells


def flux_apply(padded, coeff_pad, extra):
    center = padded[:, 1:-1, 1:-1]
    coeff_mid = coeff_pad[:, 1:-1, 1:-1]
    flux_x = coeff_mid[0] * (center - padded[:, 2:, 1:-1])
    flux_y = coeff_mid[1] * (center - padded[:, 1:-1, 2:])
    below_x = coeff_pad[0, :-2, 1:-1] * (padded[:, :-2, 1:-1] - center)
    below_y = coeff_pad[1, 1:-1, :-2] * (padded[:, 1:-1, :-2] - center)
    next_z = jnp.concatenate([center[..., 1:], jnp.zeros_like(center[..., :1])], axis=-1)
    flux_z = coeff_mid[2] * (center - next_z)
    below_z = jnp.concatenate([jnp.zeros_like(flux_z[..., :1]), flux_z[..., :-1]], axis=-1)
    return extra * center + flux_x + flux_y + flux_z - below_x - below_y - below_z


def small_solve(matrix, vector):
    lower = jnp.linalg.cholesky(matrix)
    middle = lax.linalg.triangular_solve(lower, vector[:, None], left_side=True, lower=True)
    result = lax.linalg.triangular_solve(
        lower, middle, left_side=True, lower=True, transpose_a=True
    )
    return result[:, 0]


def on_device(basis, rhs, extra_diag, coeff):
    lower_x = shifted(coeff[0][-1:], "gx", 1)
    lower_y = shifted(coeff[1][:, -1:], "gy", 1)
    coeff_pad = jnp.pad(coeff, ((0, 0), (1, 1), (1, 1), (0, 0)))
    coeff_pad = coeff_pad.at[0, 0, 1:-1].set(lower_x[0])
    coeff_pad = coeff_pad.at[1, 1:-1, 0].set(lower_y[:, 0])
    count = basis.shape[0]
    flat_basis = basis.reshape(count, -1)
    padded_basis = padded_2(basis, (("gx", 1), ("gy", 2)), 1)
    applied = flux_apply(padded_basis, coeff_pad, extra_diag)
    local_gram = jnp.dot(flat_basis, applied.reshape(count, -1).T, precision=precise)
    local_proj = jnp.dot(flat_basis, rhs.reshape(-1), precision=precise)
    gram, projected = lax.psum((local_gram, local_proj), ("gx", "gy"))
    gram = 0.5 * (gram + gram.T)
    weights = small_solve(gram, projected)
    guess = jnp.tensordot(weights, basis, axes=1, precision=precise)
    residual = rhs - jnp.tensordot(weights, applied, axes=1, precision=precise)
    coeff_mid = coeff_pad[:, 1:-1, 1:-1]
    below_kz = jnp.concatenate([jnp.zeros_like(coeff[2][..., :1]), coeff[2][..., :-1]], axis=-1)
    diagonal = (
        extra_diag
        + coeff_mid[0]
        + coeff_mid[1]
        + coeff_mid[2]
        + coeff_pad[0, :-2, 1:-1]
        + coeff_pad[1, 1:-1, :-2]
        + below_kz
    )
    direction = residual / diagonal
    direction_pad = padded_2(direction, (("gx", 0), ("gy", 1)), 1)
    applied_dir = flux_apply(direction_pad[None], coeff_pad, extra_diag)[0]
    local_corr = jnp.dot(flat_basis, applied_dir.reshape(-1), precision=precise)
    correction = lax.psum(local_corr, ("gx", "gy"))
    shift_coef = small_solve(gram, correction)
    update = direction - jnp.tensordot(shift_coef, basis, axes=1, precision=precise)
    update_pad = padded_2(update, (("gx", 0), ("gy", 1)), 1)
    applied_upd = flux_apply(update_pad[None], coeff_pad, extra_diag)[0]
    numerator, denominator = lax.psum(
        (jnp.sum(residual * update), jnp.sum(update * applied_upd)), ("gx", "gy")
    )
    step_size = numerator / denominator
    return (guess, guess + step_size * update)


def solution(mesh):
    placed = (
        P(None, "gx", "gy", None),
        P("gx", "gy", None),
        P("gx", "gy", None),
        P(None, "gx", "gy", None),
    )
    return jax.shard_map(
        on_device,
        mesh=mesh,
        in_specs=placed,
        out_specs=(P("gx", "gy", None), P("gx", "gy", None)),
        check_vma=False,
    )
```

profile of v0, /device:TPU:1, one launch (start us, length us, event | category | flops | bytes accessed | tf_op | source)
XLA Modules:
  0.0 410.9 jit_solution(2487708091433647536)
XLA Ops:
  0.6 0.7 slice_bitcast_fusion.7
  1.3 4.6 %collective-permute-start = (f32[1,8,256]{2,1,0:T(8,128)S(1)}, f32[1,8,256]{2,1,0:T(8,128)S(1)}, u32[]{:S(2)}, u32[]{:S(2)}) collective-permute-start(f32[1,8,256]{2,1,0:T(8,128)S(1)} %slice_bitcast_fusion.7), channel_id=1, source_target_pairs={{0,16},{16,32},{32,48},{48,64},{64,80},{80,96},{96,112},{112,128},... | collective-permute-start | bytes 24584 | tf_op jit(solution)/shard_map/ppermute | solution.py:12
  6.0 2.8 copy.11
  8.8 0.9 fusion.53
  9.7 1.9 collective-permute-start.3
  11.6 3.5 collective-permute-start.1
  15.2 0.0 copy-start
  15.2 2.8 collective-permute-start.2
  18.0 1.9 slice.287
  20.0 0.0 collective-permute-done
  20.0 0.2 scatter.6
  20.2 0.0 collective-permute-done.1
  20.2 0.1 scatter.9
  20.3 0.0 collective-permute-done.3
  20.3 0.0 copy-start.5
  20.3 3.0 subtract_multiply_fusion
  23.4 0.0 copy-start.4
  23.4 0.0 collective-permute-done.2
  23.4 0.1 fusion.52
  23.5 1.4 collective-permute-start.4
  24.9 4.2 %collective-permute-start.5 = (f32[32,10,1,256]{3,0,2,1:T(8,128)S(1)}, f32[32,10,1,256]{3,0,2,1:T(8,128)S(1)}, u32[]{:S(2)}, u32[]{:S(2)}) collective-permute-start(f32[32,10,1,256]{3,0,2,1:T(8,128)S(1)} %get-tuple-element.38), channel_id=1, source_target_pairs={{0,1},{1,2},{2,3},{3,4},{4,5},{5,6},{6,7},{7,8},{8,9},{9,10},{10,1... | collective-permute-start | bytes 983048 | tf_op jit(solution)/shard_map/ppermute | solution.py:23
  29.1 2.8 convolution_bitcast_fusion.6
  31.9 2.9 collective-permute-done.4
  34.8 1.8 collective-permute-done.5
  36.6 2.9 fusion.3
  39.5 1.3 copy-done.3
  40.8 2.9 convolution_bitcast_fusion
  43.7 110.2 %all-reduce.9 = (f32[32,1]{0,1:T(1,128)S(1)}, f32[32,32]{1,0:T(8,128)S(1)}) all-reduce(f32[32,1]{0,1:T(1,128)S(1)} %convolution_bitcast_fusion.6, f32[32,32]{1,0:T(8,128)S(1)} %convolution_bitcast_fusion), channel_id=1, replica_groups=mesh['gx'=32,'gy'=16] {'gx','gy'}, use_global_device_ids=true, to_apply=%region_3.0 | all-reduce | flops 1056 | bytes 8448 | tf_op jit(solution)/shard_map/psum | solution.py:66
  153.9 0.1 copy.25
  154.0 0.1 copy.26
  154.1 2.9 cholesky.18
  157.1 0.6 compare_reduce_fusion
  157.7 0.7 fusion.39
  158.4 2.4 custom-call.11
  160.8 0.2 convolution_bitcast_fusion.4
  160.9 0.1 convolution_bitcast_fusion.3
  161.1 2.7 fusion.56
  163.8 0.1 add_divide_fusion
  163.9 3.1 collective-permute-start.6
  167.0 1.9 collective-permute-start.7
  168.9 3.0 collective-permute-done.7
  172.0 3.6 collective-permute-start.8
  175.6 1.3 collective-permute-start.9
  176.9 1.2 copy.38
  178.2 1.9 collective-permute-done.9
  180.1 0.1 slice.298
  180.2 0.1 fusion.30
  180.3 0.1 copy.37
  180.4 1.7 convolution_bitcast_fusion.5
  182.1 103.9 %psum.37 = f32[32,1]{0,1:T(1,128)S(1)} all-reduce(f32[32,1]{0,1:T(1,128)S(1)} %convolution_bitcast_fusion.5), channel_id=1, replica_groups=mesh['gx'=32,'gy'=16] {'gx','gy'}, use_global_device_ids=true, to_apply=%region_4.8 | all-reduce | flops 32 | bytes 256 | tf_op jit(solution)/shard_map/psum | solution.py:86
  286.0 0.1 convolution_bitcast_fusion.2
  286.1 0.1 convolution_bitcast_fusion.1
  286.3 2.2 fusion.47
  288.5 3.7 collective-permute-start.10
  292.2 1.9 collective-permute-start.11
  294.1 3.0 collective-permute-done.11
  297.2 1.3 collective-permute-start.12
  298.5 1.5 collective-permute-start.13
  300.0 2.2 fusion.49
  302.3 0.7 collective-permute-done.13
  303.0 0.1 slice.307
  303.1 0.7 fusion.19
  303.8 105.1 %all-reduce.8 = (f32[]{:T(128)}, f32[]{:T(128)}) all-reduce(f32[]{:T(128)} %get-tuple-element.30, f32[]{:T(128)} %get-tuple-element.29), channel_id=1, replica_groups=mesh['gx'=32,'gy'=16] {'gx','gy'}, use_global_device_ids=true, to_apply=%region_6.10 | all-reduce | flops 2 | bytes 16 | tf_op jit(solution)/shard_map/psum | solution.py:91
  410.2 0.7 multiply_add_fusion
  (32 shorter events, 0.4 us)
Async XLA Ops:
  1.3 10.2 %copy-start.6 = (f32[3,8,8,256]{3,2,1,0:T(8,128)S(1)}, f32[3,8,8,256]{3,2,1,0:T(8,128)}, u32[]{:S(2)}) copy-start(f32[3,8,8,256]{3,2,1,0:T(8,128)} %param.16) | copy-start | bytes 589828
  1.3 18.7 %collective-permute-start = (f32[1,8,256]{2,1,0:T(8,128)S(1)}, f32[1,8,256]{2,1,0:T(8,128)S(1)}, u32[]{:S(2)}, u32[]{:S(2)}) collective-permute-start(f32[1,8,256]{2,1,0:T(8,128)S(1)} %slice_bitcast_fusion.7), channel_id=1, source_target_pairs={{0,16},{16,32},{32,48},{48,64},{64,80},{80,96},{96,112},{112,128},... | collective-permute-start | bytes 24584 | tf_op jit(solution)/shard_map/ppermute | solution.py:12
  8.8 11.2 %copy-start.1 = (f32[32,8,8,256]{3,0,2,1:T(8,128)}, f32[32,8,8,256]{3,0,2,1:T(8,128)S(1)}, u32[]{:S(2)}) copy-start(f32[32,8,8,256]{3,0,2,1:T(8,128)S(1)} %copy.11) | copy-start | bytes 6291460
  9.7 10.6 %collective-permute-start.3 = (f32[32,1,8,256]{3,0,2,1:T(8,128)}, f32[32,1,8,256]{3,0,2,1:T(8,128)S(1)}, u32[]{:S(2)}, u32[]{:S(2)}) collective-permute-start(f32[32,1,8,256]{3,0,2,1:T(8,128)} %get-tuple-element.42), channel_id=1, source_target_pairs={{0,16},{16,32},{32,48},{48,64},{64,80},{80,96},{96,112},{112,128},... | collective-permute-start | bytes 786440 | tf_op jit(solution)/shard_map/ppermute | solution.py:23
  11.6 8.5 %collective-permute-start.1 = (f32[8,1,256]{2,1,0:T(1,128)S(1)}, f32[8,1,256]{2,1,0:T(1,128)S(1)}, u32[]{:S(2)}, u32[]{:S(2)}) collective-permute-start(f32[8,1,256]{2,1,0:T(1,128)S(1)} %slice.280), channel_id=1, source_target_pairs={{0,1},{1,2},{2,3},{3,4},{4,5},{5,6},{6,7},{7,8},{8,9},{9,10},{10,1... | collective-permute-start | bytes 24584 | tf_op jit(solution)/shard_map/ppermute | solution.py:12
  15.2 5.1 %copy-start = (f32[32,8,8,256]{3,2,1,0:T(8,128)S(1)}, f32[32,8,8,256]{3,2,1,0:T(8,128)}, u32[]{:S(2)}) copy-start(f32[32,8,8,256]{3,2,1,0:T(8,128)} %param.13) | copy-start | bytes 6291460
  15.2 8.2 %collective-permute-start.2 = (f32[32,1,8,256]{3,0,2,1:T(8,128)}, f32[32,1,8,256]{3,0,2,1:T(8,128)S(1)}, u32[]{:S(2)}, u32[]{:S(2)}) collective-permute-start(f32[32,1,8,256]{3,0,2,1:T(8,128)} %get-tuple-element.41), channel_id=1, source_target_pairs={{16,0},{32,16},{48,32},{64,48},{80,64},{96,80},{112,96},{128,112},... | collective-permute-start | bytes 786440 | tf_op jit(solution)/shard_map/ppermute | solution.py:25
  20.3 8.8 %copy-start.5 = (f32[8,8,256]{2,1,0:T(8,128)S(1)}, f32[8,8,256]{2,1,0:T(8,128)}, u32[]{:S(2)}) copy-start(f32[8,8,256]{2,1,0:T(8,128)} %param.14) | copy-start | bytes 196612
  23.4 13.2 %copy-start.2 = (f32[32,8,8,256]{3,0,2,1:T(8,128)S(1)}, f32[32,8,8,256]{3,0,2,1:T(8,128)}, u32[]{:S(2)}) copy-start(f32[32,8,8,256]{3,0,2,1:T(8,128)} %copy-done.1) | copy-start | bytes 6291460
  23.4 13.2 %copy-start.4 = (f32[8,8,256]{2,1,0:T(8,128)S(1)}, f32[8,8,256]{2,1,0:T(8,128)}, u32[]{:S(2)}) copy-start(f32[8,8,256]{2,1,0:T(8,128)} %param.15) | copy-start | bytes 196612
  23.5 11.3 %collective-permute-start.4 = (f32[32,10,1,256]{3,0,2,1:T(8,128)S(1)}, f32[32,10,1,256]{3,0,2,1:T(8,128)S(1)}, u32[]{:S(2)}, u32[]{:S(2)}) collective-permute-start(f32[32,10,1,256]{3,0,2,1:T(8,128)S(1)} %get-tuple-element.37), channel_id=1, source_target_pairs={{1,0},{2,1},{3,2},{4,3},{5,4},{6,5},{7,6},{8,7},{9,8},{10,9},{11,1... | collective-permute-start | bytes 983048 | tf_op jit(solution)/shard_map/ppermute | solution.py:25
  24.9 11.7 %collective-permute-start.5 = (f32[32,10,1,256]{3,0,2,1:T(8,128)S(1)}, f32[32,10,1,256]{3,0,2,1:T(8,128)S(1)}, u32[]{:S(2)}, u32[]{:S(2)}) collective-permute-start(f32[32,10,1,256]{3,0,2,1:T(8,128)S(1)} %get-tuple-element.38), channel_id=1, source_target_pairs={{0,1},{1,2},{2,3},{3,4},{4,5},{5,6},{6,7},{7,8},{8,9},{9,10},{10,1... | collective-permute-start | bytes 983048 | tf_op jit(solution)/shard_map/ppermute | solution.py:23
  39.5 1.3 copy-start.3
  163.9 5.0 %collective-permute-start.6 = (f32[1,8,256]{2,1,0:T(8,128)S(1)}, f32[1,8,256]{2,1,0:T(8,128)S(1)}, u32[]{:S(2)}, u32[]{:S(2)}) collective-permute-start(f32[1,8,256]{2,1,0:T(8,128)S(1)} %get-tuple-element.56), channel_id=1, source_target_pairs={{0,16},{16,32},{32,48},{48,64},{64,80},{80,96},{96,112},{112,128},... | collective-permute-start | bytes 24584 | tf_op jit(solution)/shard_map/ppermute | solution.py:23
  167.0 5.0 %collective-permute-start.7 = (f32[1,8,256]{2,1,0:T(8,128)S(1)}, f32[1,8,256]{2,1,0:T(8,128)S(1)}, u32[]{:S(2)}, u32[]{:S(2)}) collective-permute-start(f32[1,8,256]{2,1,0:T(8,128)S(1)} %get-tuple-element.57), channel_id=1, source_target_pairs={{16,0},{32,16},{48,32},{64,48},{80,64},{96,80},{112,96},{128,112},... | collective-permute-start | bytes 24584 | tf_op jit(solution)/shard_map/ppermute | solution.py:25
  172.0 6.2 %collective-permute-start.8 = (f32[10,1,256]{2,1,0:T(1,128)S(1)}, f32[10,1,256]{2,1,0:T(1,128)S(1)}, u32[]{:S(2)}, u32[]{:S(2)}) collective-permute-start(f32[10,1,256]{2,1,0:T(1,128)S(1)} %get-tuple-element.52), channel_id=1, source_target_pairs={{0,1},{1,2},{2,3},{3,4},{4,5},{5,6},{6,7},{7,8},{8,9},{9,10},{10,1... | collective-permute-start | bytes 30728 | tf_op jit(solution)/shard_map/ppermute | solution.py:23
  175.6 4.4 %collective-permute-start.9 = (f32[10,1,256]{2,1,0:T(1,128)S(1)}, f32[10,1,256]{2,1,0:T(1,128)S(1)}, u32[]{:S(2)}, u32[]{:S(2)}) collective-permute-start(f32[10,1,256]{2,1,0:T(1,128)S(1)} %get-tuple-element.53), channel_id=1, source_target_pairs={{1,0},{2,1},{3,2},{4,3},{5,4},{6,5},{7,6},{8,7},{9,8},{10,9},{11,1... | collective-permute-start | bytes 30728 | tf_op jit(solution)/shard_map/ppermute | solution.py:25
  288.5 5.6 %collective-permute-start.10 = (f32[1,8,256]{2,1,0:T(8,128)S(1)}, f32[1,8,256]{2,1,0:T(8,128)S(1)}, u32[]{:S(2)}, u32[]{:S(2)}) collective-permute-start(f32[1,8,256]{2,1,0:T(8,128)S(1)} %get-tuple-element.54), channel_id=1, source_target_pairs={{0,16},{16,32},{32,48},{48,64},{64,80},{80,96},{96,112},{112,128},... | collective-permute-start | bytes 24584 | tf_op jit(solution)/shard_map/ppermute | solution.py:23
  292.2 5.0 %collective-permute-start.11 = (f32[1,8,256]{2,1,0:T(8,128)S(1)}, f32[1,8,256]{2,1,0:T(8,128)S(1)}, u32[]{:S(2)}, u32[]{:S(2)}) collective-permute-start(f32[1,8,256]{2,1,0:T(8,128)S(1)} %get-tuple-element.55), channel_id=1, source_target_pairs={{16,0},{32,16},{48,32},{64,48},{80,64},{96,80},{112,96},{128,112},... | collective-permute-start | bytes 24584 | tf_op jit(solution)/shard_map/ppermute | solution.py:25
  297.2 5.1 %collective-permute-start.12 = (f32[10,1,256]{2,1,0:T(1,128)S(1)}, f32[10,1,256]{2,1,0:T(1,128)S(1)}, u32[]{:S(2)}, u32[]{:S(2)}) collective-permute-start(f32[10,1,256]{2,1,0:T(1,128)S(1)} %get-tuple-element.50), channel_id=1, source_target_pairs={{0,1},{1,2},{2,3},{3,4},{4,5},{5,6},{6,7},{7,8},{8,9},{9,10},{10,1... | collective-permute-start | bytes 30728 | tf_op jit(solution)/shard_map/ppermute | solution.py:23
  298.5 4.4 %collective-permute-start.13 = (f32[10,1,256]{2,1,0:T(1,128)S(1)}, f32[10,1,256]{2,1,0:T(1,128)S(1)}, u32[]{:S(2)}, u32[]{:S(2)}) collective-permute-start(f32[10,1,256]{2,1,0:T(1,128)S(1)} %get-tuple-element.51), channel_id=1, source_target_pairs={{1,0},{2,1},{3,2},{4,3},{5,4},{6,5},{7,6},{8,7},{9,8},{10,9},{11,1... | collective-permute-start | bytes 30728 | tf_op jit(solution)/shard_map/ppermute | solution.py:25
where the time goes:
time: 412 us; the launch traced here: 411 us
  blocking collectives  319 us (77%)
  starting transfers between devices  36.8 us (9%)
  matrix products  15.1 us (4%)
  other arithmetic  14.3 us (3%)
  waiting for transfers between devices  13.3 us (3%)
  local copies, waits for them, and re-layouts  9.65 us (2%)
    psum x1, blocking collectives, on_device(): gram, projected = lax.psum((local_gram, local_proj), ('gx', 'gy'))  110 us
    psum x1, blocking collectives, on_device(): lax.psum((jnp.sum(residual * update), jnp.sum(update * applied_upd)), ('g...  105 us
    psum x1, blocking collectives, on_device(): correction = lax.psum(local_corr, ('gx', 'gy'))  104 us
    ppermute x6, starting transfers between devices, padded_2(): lax.ppermute(tail, axis, [(i, (i + 1) % count) for i in range(ends)])  17.8 us
    ppermute x6, waiting for transfers between devices, padded_2(): lax.ppermute(head, axis, [((i + 1) % count, i) for i in range(ends)])  11.5 us
    ppermute x6, starting transfers between devices, padded_2(): lax.ppermute(head, axis, [((i + 1) % count, i) for i in range(ends)])  10.9 us
  transfers between devices with their start and end apart: 14, of which 6 were waited for; matrix products, arithmetic and copies ran while one was open for 4% of the time, Pallas kernels for 0%

commit v1 on v0

v1 whole, which is shorter than its diff:
```python
import functools

import jax
import jax.numpy as jnp
from jax import lax
from jax.experimental import pallas as pl
from jax.experimental.pallas import tpu as pltpu
from jax.sharding import PartitionSpec as P

MESH = pl.DeviceIdType.MESH
F32 = jnp.float32
BF16 = jnp.bfloat16
NV = 32
BX = 8
BY = 8
BZ = 256
HZ = 128
CHUNKS = 4
ROWS = 9


def split(value):
    high = value.astype(BF16)
    low = (value - high.astype(F32)).astype(BF16)
    return high, low


def dot_t(a, b):
    return lax.dot_general(a, b, (((1,), (1,)), ((), ())), preferred_element_type=F32)


def kernel(
    n_gx,
    n_gy,
    basis_hbm,
    rhs_hbm,
    extra_hbm,
    coeff_hbm,
    guess_hbm,
    stepped_hbm,
    v_ref,
    rhs_ref,
    ext_ref,
    cf_ref,
    vh,
    vl,
    ah,
    al,
    fh,
    fl,
    gh,
    gl,
    pylo,
    pyhi,
    hxlo,
    hxup,
    hylo,
    hyup,
    cxm,
    cym,
    cpack,
    cxlo,
    cylo,
    proj_acc,
    prod,
    wb,
    g_ref,
    d_ref,
    o_ref,
    dplo,
    dphi,
    dxlo,
    dxup,
    dylo,
    dyup,
    src1,
    src2,
    a1c,
    a1x,
    a1z,
    a2c,
    a2x,
    a2z,
    load_sem,
    out_sem,
    hs_send,
    hs_recv,
    ar_send,
    ar_recv,
):
    ix = lax.axis_index("gx")
    iy = lax.axis_index("gy")
    core = ix % 2
    xy = ix // 2
    n_xy = n_gx // 2
    up_x = ((ix + 1) % n_gx, iy)
    lo_x = ((ix + n_gx - 1) % n_gx, iy)
    up_y = (ix, (iy + 1) % n_gy)
    lo_y = (ix, (iy + n_gy - 1) % n_gy)
    core_peers = [(xy * 2 + (core + 1) % 2, iy)]
    xy_peers = [(((xy + t) % n_xy) * 2 + core, iy) for t in range(1, n_xy)]
    z_peers = [(ix, (iy + t) % n_gy) for t in range(1, n_gy)]
    first_x, last_x = ix == 0, ix == n_gx - 1
    first_y, last_y = iy == 0, iy == n_gy - 1

    per = NV // CHUNKS
    loads = [
        pltpu.make_async_copy(coeff_hbm, cf_ref, load_sem.at[CHUNKS]),
        pltpu.make_async_copy(rhs_hbm, rhs_ref, load_sem.at[CHUNKS + 1]),
        pltpu.make_async_copy(extra_hbm, ext_ref, load_sem.at[CHUNKS + 2]),
    ]
    v_loads = [
        pltpu.make_async_copy(
            basis_hbm.at[pl.ds(k * per, per)], v_ref.at[pl.ds(k * per, per)], load_sem.at[k]
        )
        for k in range(CHUNKS)
    ]
    for copy in v_loads[:1] + loads + v_loads[1:]:
        copy.start()

    barrier = pltpu.get_barrier_semaphore()
    greeted = [up_x, lo_x] + z_peers + xy_peers + core_peers
    for peer in greeted:
        pl.semaphore_signal(barrier, inc=1, device_id=peer, device_id_type=MESH)
    pl.semaphore_wait(barrier, len(greeted))

    sent = []

    def send(src, dst, at, peer):
        copy = pltpu.make_async_remote_copy(
            src, dst, hs_send.at[at], hs_recv.at[at], device_id=peer, device_id_type=MESH
        )
        copy.start()
        sent.append(copy)
        return copy

    low, high = pl.ds(0, HZ), pl.ds(HZ, HZ)
    x_first = [
        send(basis_hbm.at[:, BX - 1, :, low], hxlo.at[:, :, low], 0, up_x),
        send(basis_hbm.at[:, 0, :, high], hxup.at[:, :, high], 1, lo_x),
    ]

    row = lax.broadcasted_iota(jnp.int32, (BY, BZ), 0)
    lane = lax.broadcasted_iota(jnp.int32, (BY, BZ), 1)
    zero = jnp.zeros((BY, BZ), F32)

    for k in range(CHUNKS):
        v_loads[k].wait()
        for i in range(k * per, (k + 1) * per):
            pylo[i] = v_ref[i, :, 0, :]
            pyhi[i] = v_ref[i, :, BY - 1, :]
    y_first = [
        send(pyhi.at[:, :, low], hylo.at[:, :, low], 2, up_y),
        send(pylo.at[:, :, high], hyup.at[:, :, high], 3, lo_y),
    ]
    for copy in loads:
        copy.wait()
    cpack[...] = cf_ref[1, :, BY - 1, :]
    c_sends = [
        send(cf_ref.at[0, BX - 1], cxlo, 4, up_x),
        send(cpack, cylo, 5, up_y),
    ]
    x_later = [
        send(basis_hbm.at[:, BX - 1, :, high], hxlo.at[:, :, high], 6, up_x),
        send(basis_hbm.at[:, 0, :, low], hxup.at[:, :, low], 7, lo_x),
    ]
    y_later = [
        send(pyhi.at[:, :, high], hylo.at[:, :, high], 8, up_y),
        send(pylo.at[:, :, low], hyup.at[:, :, low], 9, lo_y),
    ]

    for x in range(BX):
        cxm[x] = cf_ref[0, x] if x < BX - 1 else jnp.where(last_x, cf_ref[0, x], 0.0)
        cym[x] = jnp.where(jnp.logical_or(row < BY - 1, last_y), cf_ref[1, x], 0.0)

    def local_pair(pair, carry):
        i0 = pair * 2
        base = pl.multiple_of(pair * 16, 16)
        flux_before = [None, None]
        acc = [jnp.zeros((BY, HZ), F32) for _ in range(2)]
        cells = [v_ref[i0 + s, 0] for s in range(2)]
        for x in range(BX):
            outs = []
            nexts = []
            for s in range(2):
                v = cells[s]
                v_up = v_ref[i0 + s, x + 1] if x < BX - 1 else zero
                nexts.append(v_up)
                flux = cxm[x] * (v - v_up)
                out = ext_ref[x] * v + flux
                if x > 0:
                    out = out - flux_before[s]
                flux_before[s] = flux
                v_up = jnp.where(row == BY - 1, 0.0, pltpu.roll(v, BY - 1, 0))
                flux = cym[x] * (v - v_up)
                out = out + flux - jnp.where(row == 0, 0.0, pltpu.roll(flux, 1, 0))
                v_up = jnp.where(lane == BZ - 1, 0.0, pltpu.roll(v, BZ - 1, 1))
                flux = cf_ref[2, x] * (v - v_up)
                out = out + flux - jnp.where(lane == 0, 0.0, pltpu.roll(flux, 1, 1))
                outs.append(out)
                term = v * rhs_ref[x]
                acc[s] = acc[s] + term[:, :HZ] + term[:, HZ:]
            rows, cols = pl.ds(base, 16), pl.ds(x * BZ, BZ)
            vh[rows, cols], vl[rows, cols] = split(jnp.concatenate(cells, axis=0))
            ah[rows, cols], al[rows, cols] = split(jnp.concatenate(outs, axis=0))
            cells = nexts
        for s in range(2):
            proj_acc[i0 + s] = jnp.sum(acc[s], axis=0, keepdims=True)
        return carry

    lax.fori_loop(0, NV // 2, local_pair, 0)
    prod[...] = dot_t(vh[...], ah[...]) + dot_t(vh[...], al[...]) + dot_t(vl[...], ah[...])

    for copy in x_first + y_first + c_sends:
        copy.wait_recv()
    cxlo_v = jnp.where(first_x, 0.0, cxlo[...])
    cylo_v = jnp.where(first_y, 0.0, cylo[...])
    cx_face = jnp.concatenate(
        [cxlo_v[:, :HZ], jnp.where(last_x, 0.0, cf_ref[0, BX - 1, :, HZ:])], axis=1
    )
    cy_face = jnp.concatenate([cylo_v[:, :HZ], jnp.where(last_y, 0.0, cpack[:, HZ:])], axis=1)
    for pair in range(NV // 2):
        for at, coef in ((0, cx_face), (1, cy_face)):
            diffs = []
            flows = []
            for i in (2 * pair, 2 * pair + 1):
                if at == 0:
                    a = v_ref[i, 0, :, :HZ] - hxlo[i, :, :HZ]
                    b = v_ref[i, BX - 1, :, HZ:] - hxup[i, :, HZ:]
                else:
                    a = pylo[i, :, :HZ] - hylo[i, :, :HZ]
                    b = pyhi[i, :, HZ:] - hyup[i, :, HZ:]
                diff = jnp.concatenate([a, b], axis=1)
                diffs.append(diff)
                flows.append(diff * coef)
            rows, cols = pl.ds(16 * pair, 16), pl.ds(at * BZ, BZ)
            fh[rows, cols], fl[rows, cols] = split(jnp.concatenate(diffs, axis=0))
            gh[rows, cols], gl[rows, cols] = split(jnp.concatenate(flows, axis=0))
    total = (
        prod[...] + dot_t(fh[...], gh[...]) + dot_t(fh[...], gl[...]) + dot_t(fl[...], gh[...])
    )
    same = (
        lax.broadcasted_iota(jnp.int32, (NV * BY, NV * BY), 0) % BY
        == lax.broadcasted_iota(jnp.int32, (NV * BY, NV * BY), 1) % BY
    )
    total = jnp.where(same, total, 0.0)
    sums = jnp.sum(total.reshape(NV, BY, NV * BY), axis=1)
    wide = jnp.concatenate([sums[8 * k : 8 * k + 8] for k in range(4)], axis=1)
    s_row = lax.broadcasted_iota(jnp.int32, (4 * NV * BY, 128), 0)
    s_col = lax.broadcasted_iota(jnp.int32, (4 * NV * BY, 128), 1)
    pick = (s_row // BY == s_col).astype(F32)
    packed = jnp.dot(wide, pick, precision=lax.Precision.HIGHEST, preferred_element_type=F32)

    eye_r = lax.broadcasted_iota(jnp.int32, (NV, 128), 0)
    eye_l = lax.broadcasted_iota(jnp.int32, (NV, 128), 1)

    def to_row(col, at):
        return jnp.sum(jnp.where(eye_l == eye_r + at, col, 0.0), axis=0, keepdims=True)

    def to_col(line, at):
        return jnp.sum(jnp.where(eye_l == eye_r + at, line, 0.0), axis=1, keepdims=True)

    proj_col = jnp.sum(proj_acc[...].reshape(NV, HZ), axis=1, keepdims=True)

    ar_waits = []

    def stage(value, src, buf, at, me, peers, count):
        src[...] = value
        for peer in peers:
            pltpu.make_async_remote_copy(
                src, buf.at[me], ar_send.at[at], ar_recv.at[at], device_id=peer, device_id_type=MESH
            ).start()
        buf[me] = value
        others = buf.at[pl.ds(0, count - 1)]
        pltpu.make_async_copy(others, others, ar_recv.at[at]).wait()
        ar_waits.append((others, at))
        return jnp.sum(buf[...], axis=0)

    value = jnp.concatenate([packed, to_row(proj_col, 0)], axis=0)
    value = stage(value, src1.at[0], a1c, 0, core, core_peers, 2)
    value = stage(value, src1.at[1], a1x, 1, xy, xy_peers, n_xy)
    value = stage(value, src1.at[2], a1z, 2, iy, z_peers, n_gy)

    gram = jnp.concatenate(
        [value[0:8]] + [pltpu.roll(value[0:8], 128 - 32 * k, 1) for k in range(1, 4)], axis=0
    )
    gram = jnp.where(eye_l < NV, gram, 0.0)
    proj = to_col(value[8:9], 0)
    mat = jnp.where(eye_l == eye_r + NV, 1.0, jnp.where(eye_l == 2 * NV, proj, gram))
    for k in range(NV):
        col = jnp.broadcast_to(mat[:, k : k + 1], (NV, 128))
        pivot = mat[k : k + 1] / col[k : k + 1]
        mat = jnp.where(eye_r == k, pivot, mat - col * pivot)
    weights = mat[:, 2 * NV : 2 * NV + 1]
    inverse = jnp.where(jnp.logical_and(eye_l >= NV, eye_l < 2 * NV), mat, 0.0)
    wb[...] = jnp.broadcast_to(weights, (NV, 128))

    for copy in x_later + y_later:
        copy.wait_recv()

    def scale(i):
        line = wb[i : i + 1, :]
        return jnp.concatenate([line, line], axis=1)

    guess = [zero for _ in range(BX)]
    halo = [zero for _ in range(4)]
    for i in range(NV):
        w = scale(i)
        for x in range(BX):
            guess[x] = guess[x] + w * v_ref[i, x]
        for at, ref in enumerate((hxlo, hxup, hylo, hyup)):
            halo[at] = halo[at] + w * ref[i]

    def apply(cells, hx_lo, hx_up, hy_lo, hy_up):
        hx_up = jnp.where(last_x, 0.0, hx_up)
        hy_up = jnp.where(last_y, 0.0, hy_up)
        before = cxlo_v * (hx_lo - cells[0])
        outs = []
        for x in range(BX):
            v = cells[x]
            flux = cf_ref[0, x] * (v - (cells[x + 1] if x < BX - 1 else hx_up))
            out = ext_ref[x] * v + flux - before
            before = flux
            v_up = jnp.where(row == BY - 1, hy_up[x : x + 1], pltpu.roll(v, BY - 1, 0))
            flux = cf_ref[1, x] * (v - v_up)
            below = cylo_v[x : x + 1] * (hy_lo[x : x + 1] - v)
            out = out + flux - jnp.where(row == 0, below, pltpu.roll(flux, 1, 0))
            v_up = jnp.where(lane == BZ - 1, 0.0, pltpu.roll(v, BZ - 1, 1))
            flux = cf_ref[2, x] * (v - v_up)
            out = out + flux - jnp.where(lane == 0, 0.0, pltpu.roll(flux, 1, 1))
            outs.append(out)
        return outs

    applied = apply(guess, *halo)
    rd = zero
    for x in range(BX):
        below = cxlo_v if x == 0 else cf_ref[0, x - 1]
        diagonal = ext_ref[x] + cf_ref[0, x] + cf_ref[1, x] + cf_ref[2, x] + below
        diagonal = diagonal + jnp.where(row == 0, cylo_v[x : x + 1], pltpu.roll(cf_ref[1, x], 1, 0))
        diagonal = diagonal + jnp.where(lane == 0, 0.0, pltpu.roll(cf_ref[2, x], 1, 1))
        res = rhs_ref[x] - applied[x]
        cell = res / diagonal
        d_ref[x] = cell
        rd = rd + res * cell
        g_ref[x] = guess[x]
    dplo[...] = d_ref[:, 0, :]
    dphi[...] = d_ref[:, BY - 1, :]
    d_sends = [
        send(d_ref.at[BX - 1], dxlo, 10, up_x),
        send(d_ref.at[0], dxup, 11, lo_x),
        send(dphi, dylo, 12, up_y),
        send(dplo, dyup, 13, lo_y),
    ]
    guess_out = pltpu.make_async_copy(g_ref, guess_hbm, out_sem.at[0])
    guess_out.start()
    w_row = to_row(weights, 0)
    rest = proj - jnp.sum(gram * w_row, axis=1, keepdims=True)
    for copy in d_sends:
        copy.wait_recv()

    cells = [d_ref[x] for x in range(BX)]
    applied = apply(cells, dxlo[...], dxup[...], dylo[...], dyup[...])
    dad = zero
    for x in range(BX):
        dad = dad + cells[x] * applied[x]

    def fold(block):
        return jnp.sum(block[:, :HZ] + block[:, HZ:], axis=0, keepdims=True)

    for i in range(NV):
        acc = v_ref[i, 0] * applied[0]
        for x in range(1, BX):
            acc = acc + v_ref[i, x] * applied[x]
        proj_acc[i] = fold(acc)
    corr_col = jnp.sum(proj_acc[...].reshape(NV, HZ), axis=1, keepdims=True)
    line_at = lax.broadcasted_iota(jnp.int32, (1, 128), 1)
    value = to_row(corr_col, NV)
    value = jnp.where(line_at == 0, jnp.sum(fold(rd), axis=1, keepdims=True), value)
    value = jnp.where(line_at == 1, jnp.sum(fold(dad), axis=1, keepdims=True), value)
    value = stage(value, src2.at[0], a2c, 3, core, core_peers, 2)
    value = stage(value, src2.at[1], a2x, 4, xy, xy_peers, n_xy)
    value = stage(value, src2.at[2], a2z, 5, iy, z_peers, n_gy)

    shift = jnp.sum(inverse * value, axis=1, keepdims=True)
    wb[...] = jnp.broadcast_to(shift, (NV, 128))
    corr = to_col(value, NV)
    numerator = value[:, 0:1] - jnp.sum(shift * rest, axis=0, keepdims=True)
    denominator = value[:, 1:2] - jnp.sum(shift * corr, axis=0, keepdims=True)
    step = numerator / denominator
    update = [d_ref[x] for x in range(BX)]
    for i in range(NV):
        m = scale(i)
        for x in range(BX):
            update[x] = update[x] - m * v_ref[i, x]
    guess_out.wait()
    for x in range(BX):
        o_ref[x] = g_ref[x] + step * update[x]
    stepped_out = pltpu.make_async_copy(o_ref, stepped_hbm, out_sem.at[1])
    stepped_out.start()
    for copy in sent:
        copy.wait_send()
    for others, at in ar_waits:
        pltpu.make_async_copy(others, others, ar_send.at[at]).wait()
    stepped_out.wait()


def solution(mesh):
    n_gx, n_gy = mesh.shape["gx"], mesh.shape["gy"]
    n_xy = n_gx // 2

    def on_device(basis, rhs, extra_diag, coeff):
        vm = pltpu.VMEM
        cell = (BX, BY, BZ)
        slab = (NV, 8, BZ)
        flat = (NV * BY, BX * BZ)
        face = (NV * BY, 2 * BZ)
        anywhere = pl.BlockSpec(memory_space=pl.ANY)
        return pl.pallas_call(
            functools.partial(kernel, n_gx, n_gy),
            out_shape=[jax.ShapeDtypeStruct(cell, F32)] * 2,
            in_specs=[anywhere] * 4,
            out_specs=[anywhere] * 2,
            scratch_shapes=[
                vm((NV,) + cell, F32),
                vm(cell, F32),
                vm(cell, F32),
                vm((3,) + cell, F32),
            ]
            + [vm(flat, BF16)] * 4
            + [vm(face, BF16)] * 4
            + [vm(slab, F32)] * 6
            + [vm(cell, F32)] * 2
            + [vm((8, BZ), F32)] * 3
            + [
                vm((NV, 1, HZ), F32),
                vm((NV * BY, NV * BY), F32),
                vm((NV, 128), F32),
                vm(cell, F32),
                vm(cell, F32),
                vm(cell, F32),
            ]
            + [vm((8, BZ), F32)] * 6
            + [
                vm((3, ROWS, 128), F32),
                vm((3, 1, 128), F32),
                vm((2, ROWS, 128), F32),
                vm((n_xy, ROWS, 128), F32),
                vm((n_gy, ROWS, 128), F32),
                vm((2, 1, 128), F32),
                vm((n_xy, 1, 128), F32),
                vm((n_gy, 1, 128), F32),
                pltpu.SemaphoreType.DMA((CHUNKS + 3,)),
                pltpu.SemaphoreType.DMA((2,)),
                pltpu.SemaphoreType.DMA((14,)),
                pltpu.SemaphoreType.DMA((14,)),
                pltpu.SemaphoreType.DMA((6,)),
                pltpu.SemaphoreType.DMA((6,)),
            ],
            compiler_params=pltpu.CompilerParams(
                collective_id=0, has_side_effects=True, vmem_limit_bytes=48 << 20
            ),
        )(basis, rhs, extra_diag, coeff)

    placed = (
        P(None, "gx", "gy", None),
        P("gx", "gy", None),
        P("gx", "gy", None),
        P(None, "gx", "gy", None),
    )
    return jax.shard_map(
        on_device,
        mesh=mesh,
        in_specs=placed,
        out_specs=(P("gx", "gy", None), P("gx", "gy", None)),
        check_vma=False,
    )
```

time: 412 us -> 63.5 us (0.15)
  blocking collectives: 319 us -> 0 us
  Pallas kernels: 0 us -> 56.3 us
  starting transfers between devices: 36.8 us -> 0 us
  matrix products: 15.1 us -> 0 us
  other arithmetic: 14.3 us -> 0 us
  waiting for transfers between devices: 13.3 us -> 0 us
  local copies, waits for them, and re-layouts: 9.65 us -> 5.45 us
    psum x3 -> x0, blocking collectives: 319 us -> none  [the longest x1 110 us: on_device(): gram, projected = lax.psum((local_gram, local_proj), ('gx', 'gy'))]
    pallas_call x0 -> x1, Pallas kernels: none -> 56.3 us  [on_device(): pl.pallas_call(functools.partial(kernel, n_gx, n_gy), out_shape=[jax.Shap...]
    ppermute x14 -> x0, starting transfers between devices: 36.8 us -> none  [the longest x6 17.8 us: padded_2(): lax.ppermute(tail, axis, [(i, (i + 1) % count) for i in range(ends)])]
    dot_general x6 -> x0, matrix products: 14.6 us -> none  [the longest x1 2.88 us: on_device(): jnp.dot(flat_basis, applied.reshape(count, -1).T, precision=precise)]
    ppermute x14 -> x0, waiting for transfers between devices: 13.3 us -> none  [the longest x6 11.5 us: padded_2(): lax.ppermute(head, axis, [((i + 1) % count, i) for i in range(ends)])]
    another operation x5 -> x0, other arithmetic: 6.69 us -> none  [the longest x3 3.6 us: small_solve(): lower = jnp.linalg.cholesky(matrix)]
  transfers between devices with their start and end apart: 14 -> 0, of which waited for: 6 -> 0; matrix products, arithmetic and copies ran while one was open for 4% -> 0% of each run, Pallas kernels for 0% -> 0%
where the time goes in v1:
time: 63.5 us; the launch traced here: 62.4 us
  Pallas kernels  56.3 us (89%)
  local copies, waits for them, and re-layouts  5.45 us (9%)
  between operations  0.65 us (1%)
    pallas_call x1, Pallas kernels, on_device(): pl.pallas_call(functools.partial(kernel, n_gx, n_gy), out_shape=[jax.Shap...  56.3 us
    unnamed x10, local copies, waits for them, and re-layouts  5.45 us

profile of v1, /device:TPU:1, one launch (start us, length us, event | category | flops | bytes accessed | tf_op | source)
XLA Modules:
  0.0 62.4 jit_solution(1564778836998628297)
XLA Ops:
  0.6 0.0 copy-start
  0.6 1.6 %copy-done = f32[32,8,8,256]{3,2,1,0:T(8,128)S(1)} copy-done((f32[32,8,8,256]{3,2,1,0:T(8,128)S(1)}, f32[32,8,8,256]{3,2,1,0:T(8,128)}, u32[]{:S(2)}) %copy-start) | copy-done | bytes 2097176
  2.2 0.0 copy-start.1
  2.2 0.9 %copy-done.1 = f32[3,8,8,256]{3,2,1,0:T(8,128)S(1)} copy-done((f32[3,8,8,256]{3,2,1,0:T(8,128)S(1)}, f32[3,8,8,256]{3,2,1,0:T(8,128)}, u32[]{:S(2)}) %copy-start.1) | copy-done | bytes 196632
  3.1 0.0 copy-start.2
  3.2 0.8 %copy-done.2 = f32[8,8,256]{2,1,0:T(8,128)S(1)} copy-done((f32[8,8,256]{2,1,0:T(8,128)S(1)}, f32[8,8,256]{2,1,0:T(8,128)}, u32[]{:S(2)}) %copy-start.2) | copy-done | bytes 65560
  4.0 0.0 copy-start.3
  4.0 0.8 %copy-done.3 = f32[8,8,256]{2,1,0:T(8,128)S(1)} copy-done((f32[8,8,256]{2,1,0:T(8,128)S(1)}, f32[8,8,256]{2,1,0:T(8,128)}, u32[]{:S(2)}) %copy-start.3) | copy-done | bytes 65560
  4.8 56.3 %shard_map.59 = (f32[8,8,256]{2,1,0:T(8,128)S(1)}, f32[8,8,256]{2,1,0:T(8,128)S(1)}) custom-call(f32[32,8,8,256]{3,2,1,0:T(8,128)S(1)} %copy-done, f32[8,8,256]{2,1,0:T(8,128)S(1)} %copy-done.2, f32[8,8,256]{2,1,0:T(8,128)S(1)} %copy-done.3, f32[3,8,8,256]{3,2,1,0:T(8,128)S(1)} %copy-done.1), custom_call_target="tpu_custom_call" | custom-call | tf_op jit(solution)/shard_map/pallas_call | solution.py:418
  61.1 0.6 %copy.8 = f32[8,8,256]{2,1,0:T(8,128)} copy(f32[8,8,256]{2,1,0:T(8,128)S(1)} %get-tuple-element.4) | data formatting | bytes 131072
  61.7 0.6 %copy.9 = f32[8,8,256]{2,1,0:T(8,128)} copy(f32[8,8,256]{2,1,0:T(8,128)S(1)} %get-tuple-element.5) | data formatting | bytes 131072
Async XLA Ops:
  0.6 1.6 %copy-start = (f32[32,8,8,256]{3,2,1,0:T(8,128)S(1)}, f32[32,8,8,256]{3,2,1,0:T(8,128)}, u32[]{:S(2)}) copy-start(f32[32,8,8,256]{3,2,1,0:T(8,128)} %basis_hbm.1) | copy-start | bytes 6291460
  2.2 0.9 %copy-start.1 = (f32[3,8,8,256]{3,2,1,0:T(8,128)S(1)}, f32[3,8,8,256]{3,2,1,0:T(8,128)}, u32[]{:S(2)}) copy-start(f32[3,8,8,256]{3,2,1,0:T(8,128)} %coeff_hbm.1) | copy-start | bytes 589828
  3.1 0.8 %copy-start.2 = (f32[8,8,256]{2,1,0:T(8,128)S(1)}, f32[8,8,256]{2,1,0:T(8,128)}, u32[]{:S(2)}) copy-start(f32[8,8,256]{2,1,0:T(8,128)} %rhs_hbm.1) | copy-start | bytes 196612
  4.0 0.8 %copy-start.3 = (f32[8,8,256]{2,1,0:T(8,128)S(1)}, f32[8,8,256]{2,1,0:T(8,128)}, u32[]{:S(2)}) copy-start(f32[8,8,256]{2,1,0:T(8,128)} %extra_hbm.1) | copy-start | bytes 196612

commit v2 on v1

--- a/solution.py
+++ b/solution.py
@@ -17,6 +17,7 @@
 HZ = 128
 CHUNKS = 4
 ROWS = 9
+SIDE = 4
 
 
 def split(value):
@@ -87,16 +88,24 @@
     hs_recv,
     ar_send,
     ar_recv,
+    news,
 ):
     ix = lax.axis_index("gx")
     iy = lax.axis_index("gy")
     core = ix % 2
     xy = ix // 2
     n_xy = n_gx // 2
+    side = SIDE
     up_x = ((ix + 1) % n_gx, iy)
     lo_x = ((ix + n_gx - 1) % n_gx, iy)
     up_y = (ix, (iy + 1) % n_gy)
     lo_y = (ix, (iy + n_gy - 1) % n_gy)
+    x_at, y_at = xy % side, xy // side
+    row_peers = [((y_at * side + (x_at + t) % side) * 2 + core, iy) for t in range(1, side)]
+    column_peers = [
+        (((y_at + t) % (n_xy // side) * side + x_at) * 2 + core, iy) for t in range(1, n_xy // side)
+    ]
+    z_at = {t: (ix, (iy + n_gy + t) % n_gy) for t in (-4, -2, -1, 1, 2, 4)}
     core_peers = [(xy * 2 + (core + 1) % 2, iy)]
     xy_peers = [(((xy + t) % n_xy) * 2 + core, iy) for t in range(1, n_xy)]
     z_peers = [(ix, (iy + t) % n_gy) for t in range(1, n_gy)]
@@ -119,10 +128,28 @@
         copy.start()
 
     barrier = pltpu.get_barrier_semaphore()
-    greeted = [up_x, lo_x] + z_peers + xy_peers + core_peers
+    greeted = [up_x, lo_x] + [z_at[t] for t in (1, -1, 2, -2)]
+    greeted = greeted + row_peers + column_peers + core_peers
     for peer in greeted:
         pl.semaphore_signal(barrier, inc=1, device_id=peer, device_id_type=MESH)
+
+    row = lax.broadcasted_iota(jnp.int32, (BY, BZ), 0)
+    lane = lax.broadcasted_iota(jnp.int32, (BY, BZ), 1)
+    zero = jnp.zeros((BY, BZ), F32)
+
+    for k in range(CHUNKS):
+        v_loads[k].wait()
+        for i in range(k * per, (k + 1) * per):
+            pylo[i] = v_ref[i, :, 0, :]
+            pyhi[i] = v_ref[i, :, BY - 1, :]
+    for copy in loads:
+        copy.wait()
+    cpack[...] = cf_ref[1, :, BY - 1, :]
     pl.semaphore_wait(barrier, len(greeted))
+
+    def tell(peers, at):
+        for peer in peers:
+            pl.semaphore_signal(news.at[at], inc=1, device_id=peer, device_id_type=MESH)
 
     sent = []
 
@@ -135,31 +162,21 @@
         return copy
 
     low, high = pl.ds(0, HZ), pl.ds(HZ, HZ)
+    y_first = [
+        send(pyhi.at[:, :, low], hylo.at[:, :, low], 2, up_y),
+        send(pylo.at[:, :, high], hyup.at[:, :, high], 3, lo_y),
+    ]
     x_first = [
         send(basis_hbm.at[:, BX - 1, :, low], hxlo.at[:, :, low], 0, up_x),
         send(basis_hbm.at[:, 0, :, high], hxup.at[:, :, high], 1, lo_x),
     ]
 
-    row = lax.broadcasted_iota(jnp.int32, (BY, BZ), 0)
-    lane = lax.broadcasted_iota(jnp.int32, (BY, BZ), 1)
-    zero = jnp.zeros((BY, BZ), F32)
-
-    for k in range(CHUNKS):
-        v_loads[k].wait()
-        for i in range(k * per, (k + 1) * per):
-            pylo[i] = v_ref[i, :, 0, :]
-            pyhi[i] = v_ref[i, :, BY - 1, :]
-    y_first = [
-        send(pyhi.at[:, :, low], hylo.at[:, :, low], 2, up_y),
-        send(pylo.at[:, :, high], hyup.at[:, :, high], 3, lo_y),
-    ]
-    for copy in loads:
-        copy.wait()
-    cpack[...] = cf_ref[1, :, BY - 1, :]
     c_sends = [
         send(cf_ref.at[0, BX - 1], cxlo, 4, up_x),
         send(cpack, cylo, 5, up_y),
     ]
+    tell(row_peers, 0)
+    tell([z_at[2], z_at[-2]], 1)
     x_later = [
         send(basis_hbm.at[:, BX - 1, :, high], hxlo.at[:, :, high], 6, up_x),
         send(basis_hbm.at[:, 0, :, low], hxup.at[:, :, low], 7, lo_x),
@@ -209,6 +226,9 @@
         return carry
 
     lax.fori_loop(0, NV // 2, local_pair, 0)
+    pl.semaphore_wait(news.at[0], len(row_peers))
+    pl.semaphore_wait(news.at[1], 2)
+    tell([z_at[4], z_at[-4]], 2)
     prod[...] = dot_t(vh[...], ah[...]) + dot_t(vh[...], al[...]) + dot_t(vl[...], ah[...])
 
     for copy in x_first + y_first + c_sends:
@@ -279,6 +299,7 @@
     value = jnp.concatenate([packed, to_row(proj_col, 0)], axis=0)
     value = stage(value, src1.at[0], a1c, 0, core, core_peers, 2)
     value = stage(value, src1.at[1], a1x, 1, xy, xy_peers, n_xy)
+    pl.semaphore_wait(news.at[2], 2)
     value = stage(value, src1.at[2], a1z, 2, iy, z_peers, n_gy)
 
     gram = jnp.concatenate(
@@ -455,9 +476,10 @@
                 pltpu.SemaphoreType.DMA((14,)),
                 pltpu.SemaphoreType.DMA((6,)),
                 pltpu.SemaphoreType.DMA((6,)),
+                pltpu.SemaphoreType.REGULAR((3,)),
             ],
             compiler_params=pltpu.CompilerParams(
-                collective_id=0, has_side_effects=True, vmem_limit_bytes=48 << 20
+                collective_id=0, has_side_effects=True, vmem_limit_bytes=63 << 20
             ),
         )(basis, rhs, extra_diag, coeff)
 

time: 63.5 us -> 57.5 us (0.906)
  Pallas kernels: 56.3 us -> 52.9 us
  local copies, waits for them, and re-layouts: 5.45 us -> 2.95 us
    pallas_call x1, Pallas kernels: 56.3 us -> 52.9 us  [on_device(): pl.pallas_call(functools.partial(kernel, n_gx, n_gy), out_shape=[jax.Shap...]
    unnamed x10 -> x2, local copies, waits for them, and re-layouts: 5.45 us -> 2.95 us
where the time goes in v2:
time: 57.5 us; the launch traced here: 56.5 us
  Pallas kernels  52.9 us (92%)
  local copies, waits for them, and re-layouts  2.95 us (5%)
  between operations  0.64 us (1%)
    pallas_call x1, Pallas kernels, on_device(): pl.pallas_call(functools.partial(kernel, n_gx, n_gy), out_shape=[jax.Shap...  52.9 us
    unnamed x2, local copies, waits for them, and re-layouts  2.95 us

profile of v2, /device:TPU:1, one launch (start us, length us, event | category | flops | bytes accessed | tf_op | source)
XLA Modules:
  0.0 56.5 jit_solution(2882714205756807187)
XLA Ops:
  0.6 52.9 %shard_map.59 = (f32[8,8,256]{2,1,0:T(8,128)}, f32[8,8,256]{2,1,0:T(8,128)}) custom-call(f32[32,8,8,256]{3,2,1,0:T(8,128)} %basis_hbm.1, f32[8,8,256]{2,1,0:T(8,128)} %rhs_hbm.1, f32[8,8,256]{2,1,0:T(8,128)} %extra_hbm.1, f32[3,8,8,256]{3,2,1,0:T(8,128)} %coeff_hbm.1), custom_call_target="tpu_custom_call" | custom-call | tf_op jit(solution)/shard_map/pallas_call | solution.py:439
  53.6 1.5 %copy.8 = f32[8,8,256]{2,1,0:T(8,128)} copy(f32[8,8,256]{2,1,0:T(8,128)} %get-tuple-element.4) | data formatting | bytes 131072
  55.0 1.5 %copy.9 = f32[8,8,256]{2,1,0:T(8,128)} copy(f32[8,8,256]{2,1,0:T(8,128)} %get-tuple-element.5) | data formatting | bytes 131072

commit v3 on v2

--- a/solution.py
+++ b/solution.py
@@ -18,6 +18,8 @@
 CHUNKS = 4
 ROWS = 9
 SIDE = 4
+PIVOTS = 4
+EARLY = 4
 
 
 def split(value):
@@ -37,8 +39,8 @@
     rhs_hbm,
     extra_hbm,
     coeff_hbm,
-    guess_hbm,
-    stepped_hbm,
+    g_ref,
+    o_ref,
     v_ref,
     rhs_ref,
     ext_ref,
@@ -65,9 +67,7 @@
     proj_acc,
     prod,
     wb,
-    g_ref,
     d_ref,
-    o_ref,
     dplo,
     dphi,
     dxlo,
@@ -83,7 +83,6 @@
     a2x,
     a2z,
     load_sem,
-    out_sem,
     hs_send,
     hs_recv,
     ar_send,
@@ -137,58 +136,10 @@
     lane = lax.broadcasted_iota(jnp.int32, (BY, BZ), 1)
     zero = jnp.zeros((BY, BZ), F32)
 
-    for k in range(CHUNKS):
-        v_loads[k].wait()
-        for i in range(k * per, (k + 1) * per):
-            pylo[i] = v_ref[i, :, 0, :]
-            pyhi[i] = v_ref[i, :, BY - 1, :]
-    for copy in loads:
-        copy.wait()
-    cpack[...] = cf_ref[1, :, BY - 1, :]
-    pl.semaphore_wait(barrier, len(greeted))
-
-    def tell(peers, at):
-        for peer in peers:
-            pl.semaphore_signal(news.at[at], inc=1, device_id=peer, device_id_type=MESH)
-
-    sent = []
-
-    def send(src, dst, at, peer):
-        copy = pltpu.make_async_remote_copy(
-            src, dst, hs_send.at[at], hs_recv.at[at], device_id=peer, device_id_type=MESH
-        )
-        copy.start()
-        sent.append(copy)
-        return copy
-
-    low, high = pl.ds(0, HZ), pl.ds(HZ, HZ)
-    y_first = [
-        send(pyhi.at[:, :, low], hylo.at[:, :, low], 2, up_y),
-        send(pylo.at[:, :, high], hyup.at[:, :, high], 3, lo_y),
-    ]
-    x_first = [
-        send(basis_hbm.at[:, BX - 1, :, low], hxlo.at[:, :, low], 0, up_x),
-        send(basis_hbm.at[:, 0, :, high], hxup.at[:, :, high], 1, lo_x),
-    ]
-
-    c_sends = [
-        send(cf_ref.at[0, BX - 1], cxlo, 4, up_x),
-        send(cpack, cylo, 5, up_y),
-    ]
-    tell(row_peers, 0)
-    tell([z_at[2], z_at[-2]], 1)
-    x_later = [
-        send(basis_hbm.at[:, BX - 1, :, high], hxlo.at[:, :, high], 6, up_x),
-        send(basis_hbm.at[:, 0, :, low], hxup.at[:, :, low], 7, lo_x),
-    ]
-    y_later = [
-        send(pyhi.at[:, :, high], hylo.at[:, :, high], 8, up_y),
-        send(pylo.at[:, :, low], hyup.at[:, :, low], 9, lo_y),
-    ]
-
-    for x in range(BX):
-        cxm[x] = cf_ref[0, x] if x < BX - 1 else jnp.where(last_x, cf_ref[0, x], 0.0)
-        cym[x] = jnp.where(jnp.logical_or(row < BY - 1, last_y), cf_ref[1, x], 0.0)
+    def coefficient_masks():
+        for x in range(BX):
+            cxm[x] = cf_ref[0, x] if x < BX - 1 else jnp.where(last_x, cf_ref[0, x], 0.0)
+            cym[x] = jnp.where(jnp.logical_or(row < BY - 1, last_y), cf_ref[1, x], 0.0)
 
     def local_pair(pair, carry):
         i0 = pair * 2
@@ -225,7 +176,58 @@
             proj_acc[i0 + s] = jnp.sum(acc[s], axis=0, keepdims=True)
         return carry
 
-    lax.fori_loop(0, NV // 2, local_pair, 0)
+    for k in range(CHUNKS):
+        v_loads[k].wait()
+        for i in range(k * per, (k + 1) * per):
+            pylo[i] = v_ref[i, :, 0, :]
+            pyhi[i] = v_ref[i, :, BY - 1, :]
+    for copy in loads:
+        copy.wait()
+    cpack[...] = cf_ref[1, :, BY - 1, :]
+    coefficient_masks()
+    lax.fori_loop(0, EARLY, local_pair, 0)
+    pl.semaphore_wait(barrier, len(greeted))
+
+    def tell(peers, at):
+        for peer in peers:
+            pl.semaphore_signal(news.at[at], inc=1, device_id=peer, device_id_type=MESH)
+
+    sent = []
+
+    def send(src, dst, at, peer):
+        copy = pltpu.make_async_remote_copy(
+            src, dst, hs_send.at[at], hs_recv.at[at], device_id=peer, device_id_type=MESH
+        )
+        copy.start()
+        sent.append(copy)
+        return copy
+
+    low, high = pl.ds(0, HZ), pl.ds(HZ, HZ)
+    y_first = [
+        send(pyhi.at[:, :, low], hylo.at[:, :, low], 2, up_y),
+        send(pylo.at[:, :, high], hyup.at[:, :, high], 3, lo_y),
+    ]
+    x_first = [
+        send(basis_hbm.at[:, BX - 1, :, low], hxlo.at[:, :, low], 0, up_x),
+        send(basis_hbm.at[:, 0, :, high], hxup.at[:, :, high], 1, lo_x),
+    ]
+
+    c_sends = [
+        send(cf_ref.at[0, BX - 1], cxlo, 4, up_x),
+        send(cpack, cylo, 5, up_y),
+    ]
+    tell(row_peers, 0)
+    tell([z_at[2], z_at[-2]], 1)
+    x_later = [
+        send(basis_hbm.at[:, BX - 1, :, high], hxlo.at[:, :, high], 6, up_x),
+        send(basis_hbm.at[:, 0, :, low], hxup.at[:, :, low], 7, lo_x),
+    ]
+    y_later = [
+        send(pyhi.at[:, :, high], hylo.at[:, :, high], 8, up_y),
+        send(pylo.at[:, :, low], hyup.at[:, :, low], 9, lo_y),
+    ]
+
+    lax.fori_loop(EARLY, NV // 2, local_pair, 0)
     pl.semaphore_wait(news.at[0], len(row_peers))
     pl.semaphore_wait(news.at[1], 2)
     tell([z_at[4], z_at[-4]], 2)
@@ -308,10 +310,24 @@
     gram = jnp.where(eye_l < NV, gram, 0.0)
     proj = to_col(value[8:9], 0)
     mat = jnp.where(eye_l == eye_r + NV, 1.0, jnp.where(eye_l == 2 * NV, proj, gram))
-    for k in range(NV):
-        col = jnp.broadcast_to(mat[:, k : k + 1], (NV, 128))
-        pivot = mat[k : k + 1] / col[k : k + 1]
-        mat = jnp.where(eye_r == k, pivot, mat - col * pivot)
+    for k in range(0, NV, PIVOTS):
+        cols = [jnp.broadcast_to(mat[:, k + j : k + j + 1], (NV, 128)) for j in range(PIVOTS)]
+        rows = [mat[k + j : k + j + 1] for j in range(PIVOTS)]
+        head = [[cols[j][k + i : k + i + 1] for j in range(PIVOTS)] for i in range(PIVOTS)]
+        for j in range(PIVOTS):
+            scaled = 1.0 / head[j][j]
+            rows[j] = rows[j] * scaled
+            for m in range(j + 1, PIVOTS):
+                head[j][m] = head[j][m] * scaled
+            for i in range(PIVOTS):
+                if i != j:
+                    rows[i] = rows[i] - head[i][j] * rows[j]
+                    for m in range(j + 1, PIVOTS):
+                        head[i][m] = head[i][m] - head[i][j] * head[j][m]
+        for j in range(PIVOTS):
+            mat = mat - cols[j] * rows[j]
+        for j in range(PIVOTS):
+            mat = jnp.where(eye_r == k + j, rows[j], mat)
     weights = mat[:, 2 * NV : 2 * NV + 1]
     inverse = jnp.where(jnp.logical_and(eye_l >= NV, eye_l < 2 * NV), mat, 0.0)
     wb[...] = jnp.broadcast_to(weights, (NV, 128))
@@ -363,7 +379,7 @@
         cell = res / diagonal
         d_ref[x] = cell
         rd = rd + res * cell
-        g_ref[x] = guess[x]
+        g_ref[x] = 0.5 * guess[x]
     dplo[...] = d_ref[:, 0, :]
     dphi[...] = d_ref[:, BY - 1, :]
     d_sends = [
@@ -372,8 +388,6 @@
         send(dphi, dylo, 12, up_y),
         send(dplo, dyup, 13, lo_y),
     ]
-    guess_out = pltpu.make_async_copy(g_ref, guess_hbm, out_sem.at[0])
-    guess_out.start()
     w_row = to_row(weights, 0)
     rest = proj - jnp.sum(gram * w_row, axis=1, keepdims=True)
     for copy in d_sends:
@@ -413,16 +427,12 @@
         m = scale(i)
         for x in range(BX):
             update[x] = update[x] - m * v_ref[i, x]
-    guess_out.wait()
     for x in range(BX):
-        o_ref[x] = g_ref[x] + step * update[x]
-    stepped_out = pltpu.make_async_copy(o_ref, stepped_hbm, out_sem.at[1])
-    stepped_out.start()
+        o_ref[x] = step * update[x]
     for copy in sent:
         copy.wait_send()
     for others, at in ar_waits:
         pltpu.make_async_copy(others, others, ar_send.at[at]).wait()
-    stepped_out.wait()
 
 
 def solution(mesh):
@@ -436,11 +446,11 @@
         flat = (NV * BY, BX * BZ)
         face = (NV * BY, 2 * BZ)
         anywhere = pl.BlockSpec(memory_space=pl.ANY)
-        return pl.pallas_call(
+        half, change = pl.pallas_call(
             functools.partial(kernel, n_gx, n_gy),
-            out_shape=[jax.ShapeDtypeStruct(cell, F32)] * 2,
+            out_shape=[vm(cell, F32)] * 2,
             in_specs=[anywhere] * 4,
-            out_specs=[anywhere] * 2,
+            out_specs=[pl.BlockSpec(memory_space=vm)] * 2,
             scratch_shapes=[
                 vm((NV,) + cell, F32),
                 vm(cell, F32),
@@ -457,8 +467,6 @@
                 vm((NV * BY, NV * BY), F32),
                 vm((NV, 128), F32),
                 vm(cell, F32),
-                vm(cell, F32),
-                vm(cell, F32),
             ]
             + [vm((8, BZ), F32)] * 6
             + [
@@ -471,7 +479,6 @@
                 vm((n_xy, 1, 128), F32),
                 vm((n_gy, 1, 128), F32),
                 pltpu.SemaphoreType.DMA((CHUNKS + 3,)),
-                pltpu.SemaphoreType.DMA((2,)),
                 pltpu.SemaphoreType.DMA((14,)),
                 pltpu.SemaphoreType.DMA((14,)),
                 pltpu.SemaphoreType.DMA((6,)),
@@ -482,6 +489,7 @@
                 collective_id=0, has_side_effects=True, vmem_limit_bytes=63 << 20
             ),
         )(basis, rhs, extra_diag, coeff)
+        return 2.0 * half, 2.0 * half + change
 
     placed = (
         P(None, "gx", "gy", None),

time: 57.5 us -> 53.3 us (0.927)
  local copies, waits for them, and re-layouts: 2.95 us -> 0 us
  Pallas kernels: 52.9 us -> 51.1 us
  other arithmetic: 0 us -> 0.66 us
    unnamed x2 -> x0, local copies, waits for them, and re-layouts: 2.95 us -> none
    pallas_call x1, Pallas kernels: 52.9 us -> 51.1 us  [on_device(): pl.pallas_call(functools.partial(kernel, n_gx, n_gy), out_shape=[vm(cell,...]
    add x0 -> x1, other arithmetic: none -> 0.66 us  [on_device(): return (2.0 * half, 2.0 * half + change)]
where the time goes in v3:
time: 53.3 us; the launch traced here: 52.4 us
  Pallas kernels  51.1 us (96%)
  other arithmetic  0.66 us (1%)
  between operations  0.64 us (1%)
    pallas_call x1, Pallas kernels, on_device(): pl.pallas_call(functools.partial(kernel, n_gx, n_gy), out_shape=[vm(cell,...  51.1 us

profile of v3, /device:TPU:1, one launch (start us, length us, event | category | flops | bytes accessed | tf_op | source)
XLA Modules:
  0.0 52.4 jit_solution(7652224021316048318)
XLA Ops:
  0.6 51.1 %shard_map.59 = (f32[8,8,256]{2,1,0:T(8,128)S(1)}, f32[8,8,256]{2,1,0:T(8,128)S(1)}) custom-call(f32[32,8,8,256]{3,2,1,0:T(8,128)} %basis_hbm.1, f32[8,8,256]{2,1,0:T(8,128)} %rhs_hbm.1, f32[8,8,256]{2,1,0:T(8,128)} %extra_hbm.1, f32[3,8,8,256]{3,2,1,0:T(8,128)} %coeff_hbm.1), custom_call_target="tpu_custom_call" | custom-call | tf_op jit(solution)/shard_map/pallas_call | solution.py:449
  51.7 0.7 %fusion = (f32[8,8,256]{2,1,0:T(8,128)}, f32[8,8,256]{2,1,0:T(8,128)}) fusion(f32[8,8,256]{2,1,0:T(8,128)S(1)} %get-tuple-element.5, f32[8,8,256]{2,1,0:T(8,128)S(1)} %get-tuple-element.4), kind=kLoop, calls=%fused_computation.1 | loop fusion | flops 32768 | bytes 262144 | tf_op jit(solution)/shard_map/add | solution.py:492

commit v4 on v3

--- a/solution.py
+++ b/solution.py
@@ -19,7 +19,6 @@
 ROWS = 9
 SIDE = 4
 PIVOTS = 4
-EARLY = 4
 
 
 def split(value):
@@ -185,7 +184,6 @@
         copy.wait()
     cpack[...] = cf_ref[1, :, BY - 1, :]
     coefficient_masks()
-    lax.fori_loop(0, EARLY, local_pair, 0)
     pl.semaphore_wait(barrier, len(greeted))
 
     def tell(peers, at):
@@ -218,16 +216,8 @@
     ]
     tell(row_peers, 0)
     tell([z_at[2], z_at[-2]], 1)
-    x_later = [
-        send(basis_hbm.at[:, BX - 1, :, high], hxlo.at[:, :, high], 6, up_x),
-        send(basis_hbm.at[:, 0, :, low], hxup.at[:, :, low], 7, lo_x),
-    ]
-    y_later = [
-        send(pyhi.at[:, :, high], hylo.at[:, :, high], 8, up_y),
-        send(pylo.at[:, :, low], hyup.at[:, :, low], 9, lo_y),
-    ]
-
-    lax.fori_loop(EARLY, NV // 2, local_pair, 0)
+
+    lax.fori_loop(0, NV // 2, local_pair, 0)
     pl.semaphore_wait(news.at[0], len(row_peers))
     pl.semaphore_wait(news.at[1], 2)
     tell([z_at[4], z_at[-4]], 2)
@@ -235,6 +225,14 @@
 
     for copy in x_first + y_first + c_sends:
         copy.wait_recv()
+    x_later = [
+        send(basis_hbm.at[:, BX - 1, :, high], hxlo.at[:, :, high], 6, up_x),
+        send(basis_hbm.at[:, 0, :, low], hxup.at[:, :, low], 7, lo_x),
+    ]
+    y_later = [
+        send(pyhi.at[:, :, high], hylo.at[:, :, high], 8, up_y),
+        send(pylo.at[:, :, low], hyup.at[:, :, low], 9, lo_y),
+    ]
     cxlo_v = jnp.where(first_x, 0.0, cxlo[...])
     cylo_v = jnp.where(first_y, 0.0, cylo[...])
     cx_face = jnp.concatenate(

time: 53.3 us -> 51.7 us (0.970); the launches traced: 52.4 us -> 51.6 us
  Pallas kernels: 51.1 us -> 50.3 us
    pallas_call x1, Pallas kernels: 51.1 us -> 50.3 us  [on_device(): pl.pallas_call(functools.partial(kernel, n_gx, n_gy), out_shape=[vm(cell,...]
where the time goes in v4:
time: 51.7 us; the launch traced here: 51.6 us
  Pallas kernels  50.3 us (97%)
  other arithmetic  0.66 us (1%)
  between operations  0.64 us (1%)
    pallas_call x1, Pallas kernels, on_device(): pl.pallas_call(functools.partial(kernel, n_gx, n_gy), out_shape=[vm(cell,...  50.3 us

profile of v4, /device:TPU:1, one launch (start us, length us, event | category | flops | bytes accessed | tf_op | source)
XLA Modules:
  0.0 51.6 jit_solution(13164998247433321155)
XLA Ops:
  0.6 50.3 %shard_map.59 = (f32[8,8,256]{2,1,0:T(8,128)S(1)}, f32[8,8,256]{2,1,0:T(8,128)S(1)}) custom-call(f32[32,8,8,256]{3,2,1,0:T(8,128)} %basis_hbm.1, f32[8,8,256]{2,1,0:T(8,128)} %rhs_hbm.1, f32[8,8,256]{2,1,0:T(8,128)} %extra_hbm.1, f32[3,8,8,256]{3,2,1,0:T(8,128)} %coeff_hbm.1), custom_call_target="tpu_custom_call" | custom-call | tf_op jit(solution)/shard_map/pallas_call | solution.py:447
  50.9 0.7 %fusion = (f32[8,8,256]{2,1,0:T(8,128)}, f32[8,8,256]{2,1,0:T(8,128)}) fusion(f32[8,8,256]{2,1,0:T(8,128)S(1)} %get-tuple-element.5, f32[8,8,256]{2,1,0:T(8,128)S(1)} %get-tuple-element.4), kind=kLoop, calls=%fused_computation.1 | loop fusion | flops 32768 | bytes 262144 | tf_op jit(solution)/shard_map/add | solution.py:490

commit v5 on v4

--- a/solution.py
+++ b/solution.py
@@ -69,10 +69,11 @@
     d_ref,
     dplo,
     dphi,
-    dxlo,
-    dxup,
-    dylo,
-    dyup,
+    bc,
+    sx,
+    sy,
+    qx,
+    qy,
     src1,
     src2,
     a1c,
@@ -282,15 +283,103 @@
 
     proj_col = jnp.sum(proj_acc[...].reshape(NV, HZ), axis=1, keepdims=True)
 
+    def turned(v, low_edge, high_edge):
+        return (
+            jnp.where(row == 0, low_edge, pltpu.roll(v, 1, 0)),
+            jnp.where(row == BY - 1, high_edge, pltpu.roll(v, BY - 1, 0)),
+        )
+
+    def along_z(v):
+        return (
+            jnp.where(lane == 0, 0.0, pltpu.roll(v, 1, 1)),
+            jnp.where(lane == BZ - 1, 0.0, pltpu.roll(v, BZ - 1, 1)),
+        )
+
+    def edge(a):
+        return 0 if a == 0 else BX - 1
+
+    q_sends = []
+
+    def boundary():
+        for copy in x_later + y_later:
+            copy.wait_recv()
+        rights = []
+        for side_at in range(2):
+            a = edge(side_at)
+            x_low = cxlo_v if a == 0 else cf_ref[0, a - 1]
+            y_low = turned(cf_ref[1, a], cylo_v[a : a + 1], 0.0)[0]
+            z_low = along_z(cf_ref[2, a])[0]
+            faces = [x_low, cf_ref[0, a], y_low, cf_ref[1, a], z_low, cf_ref[2, a]]
+            faces.append(ext_ref[a])
+            inverse_d = 1.0 / sum(faces[1:], faces[0])
+            for m, face in enumerate(faces):
+                bc[side_at, m] = face
+            bc[side_at, 7] = inverse_d
+            rights.append(rhs_ref[a] * inverse_d)
+        for side_at in range(2):
+            b = edge(side_at)
+            c_x = cf_ref[0, :, b, :]
+            x_low = turned(c_x, cxlo_v[b : b + 1], 0.0)[0]
+            y_low = cylo_v if b == 0 else cf_ref[1, :, b - 1, :]
+            c_z = cf_ref[2, :, b, :]
+            faces = [x_low, c_x, y_low, cf_ref[1, :, b, :], along_z(c_z)[0], c_z]
+            faces.append(ext_ref[:, b, :])
+            inverse_d = 1.0 / sum(faces[1:], faces[0])
+            for m, face in enumerate(faces):
+                bc[2 + side_at, m] = face
+            bc[2 + side_at, 7] = inverse_d
+            rights.append(rhs_ref[:, b, :] * inverse_d)
+
+        def meet(at, v, near):
+            out = bc[at, 6] * v
+            for m, other in enumerate(near):
+                out = out + bc[at, m] * (v - other)
+            return out * bc[at, 7]
+
+        def one(i, carry):
+            x_lo, y_lo = hxlo[i], hylo[i]
+            x_up = jnp.where(last_x, 0.0, hxup[i])
+            y_up = jnp.where(last_y, 0.0, hyup[i])
+            found = []
+            for at in range(2):
+                a = edge(at)
+                v = v_ref[i, a]
+                x_near = (x_lo, v_ref[i, 1]) if a == 0 else (v_ref[i, a - 1], x_up)
+                y_near = turned(v, y_lo[a : a + 1], y_up[a : a + 1])
+                found.append(meet(at, v, x_near + y_near + along_z(v)))
+            for at in range(2):
+                b = edge(at)
+                v = pylo[i] if b == 0 else pyhi[i]
+                y_near = (y_lo, v_ref[i, :, 1, :]) if b == 0 else (v_ref[i, :, b - 1, :], y_up)
+                x_near = turned(v, x_lo[b : b + 1], x_up[b : b + 1])
+                found.append(meet(2 + at, v, x_near + y_near + along_z(v)))
+            sx[i] = jnp.concatenate([found[1][:, :HZ], found[0][:, HZ:]], axis=1)
+            sy[i] = jnp.concatenate([found[3][:, :HZ], found[2][:, HZ:]], axis=1)
+            return carry
+
+        lax.fori_loop(0, NV, one, 0)
+        sx[NV] = jnp.concatenate([rights[1][:, :HZ], rights[0][:, HZ:]], axis=1)
+        sy[NV] = jnp.concatenate([rights[3][:, :HZ], rights[2][:, HZ:]], axis=1)
+        q_sends.extend(
+            [
+                send(sy.at[:, :, low], qy.at[:, :, low], 12, up_y),
+                send(sy.at[:, :, high], qy.at[:, :, high], 13, lo_y),
+                send(sx.at[:, :, low], qx.at[:, :, low], 10, up_x),
+                send(sx.at[:, :, high], qx.at[:, :, high], 11, lo_x),
+            ]
+        )
+
     ar_waits = []
 
-    def stage(value, src, buf, at, me, peers, count):
+    def stage(value, src, buf, at, me, peers, count, meanwhile=None):
         src[...] = value
         for peer in peers:
             pltpu.make_async_remote_copy(
                 src, buf.at[me], ar_send.at[at], ar_recv.at[at], device_id=peer, device_id_type=MESH
             ).start()
         buf[me] = value
+        if meanwhile is not None:
+            meanwhile()
         others = buf.at[pl.ds(0, count - 1)]
         pltpu.make_async_copy(others, others, ar_recv.at[at]).wait()
         ar_waits.append((others, at))
@@ -300,7 +389,7 @@
     value = stage(value, src1.at[0], a1c, 0, core, core_peers, 2)
     value = stage(value, src1.at[1], a1x, 1, xy, xy_peers, n_xy)
     pl.semaphore_wait(news.at[2], 2)
-    value = stage(value, src1.at[2], a1z, 2, iy, z_peers, n_gy)
+    value = stage(value, src1.at[2], a1z, 2, iy, z_peers, n_gy, boundary)
 
     gram = jnp.concatenate(
         [value[0:8]] + [pltpu.roll(value[0:8], 128 - 32 * k, 1) for k in range(1, 4)], axis=0
@@ -330,7 +419,7 @@
     inverse = jnp.where(jnp.logical_and(eye_l >= NV, eye_l < 2 * NV), mat, 0.0)
     wb[...] = jnp.broadcast_to(weights, (NV, 128))
 
-    for copy in x_later + y_later:
+    for copy in q_sends:
         copy.wait_recv()
 
     def scale(i):
@@ -339,12 +428,14 @@
 
     guess = [zero for _ in range(BX)]
     halo = [zero for _ in range(4)]
+    beyond = [qx[NV], qy[NV]]
     for i in range(NV):
         w = scale(i)
         for x in range(BX):
             guess[x] = guess[x] + w * v_ref[i, x]
         for at, ref in enumerate((hxlo, hxup, hylo, hyup)):
             halo[at] = halo[at] + w * ref[i]
+        beyond = [beyond[0] - w * qx[i], beyond[1] - w * qy[i]]
 
     def apply(cells, hx_lo, hx_up, hy_lo, hy_up):
         hx_up = jnp.where(last_x, 0.0, hx_up)
@@ -366,6 +457,21 @@
             outs.append(out)
         return outs
 
+    def apply_inside(cells):
+        before = zero
+        outs = []
+        for x in range(BX):
+            v = cells[x]
+            flux = cxm[x] * (v - (cells[x + 1] if x < BX - 1 else zero))
+            out = ext_ref[x] * v + flux - before
+            before = flux
+            flux = cym[x] * (v - turned(v, 0.0, 0.0)[1])
+            out = out + flux - turned(flux, 0.0, 0.0)[0]
+            flux = cf_ref[2, x] * (v - along_z(v)[1])
+            out = out + flux - along_z(flux)[0]
+            outs.append(out)
+        return outs
+
     applied = apply(guess, *halo)
     rd = zero
     for x in range(BX):
@@ -380,20 +486,15 @@
         g_ref[x] = 0.5 * guess[x]
     dplo[...] = d_ref[:, 0, :]
     dphi[...] = d_ref[:, BY - 1, :]
-    d_sends = [
-        send(d_ref.at[BX - 1], dxlo, 10, up_x),
-        send(d_ref.at[0], dxup, 11, lo_x),
-        send(dphi, dylo, 12, up_y),
-        send(dplo, dyup, 13, lo_y),
-    ]
     w_row = to_row(weights, 0)
     rest = proj - jnp.sum(gram * w_row, axis=1, keepdims=True)
-    for copy in d_sends:
-        copy.wait_recv()
 
     cells = [d_ref[x] for x in range(BX)]
-    applied = apply(cells, dxlo[...], dxup[...], dylo[...], dyup[...])
-    dad = zero
+    applied = apply_inside(cells)
+    jump_x = jnp.concatenate([cells[0][:, :HZ], cells[BX - 1][:, HZ:]], axis=1) - beyond[0]
+    jump_y = jnp.concatenate([dplo[:, :HZ], dphi[:, HZ:]], axis=1) - beyond[1]
+    flow_x, flow_y = cx_face * jump_x, cy_face * jump_y
+    dad = flow_x * jump_x + flow_y * jump_y
     for x in range(BX):
         dad = dad + cells[x] * applied[x]
 
@@ -404,6 +505,10 @@
         acc = v_ref[i, 0] * applied[0]
         for x in range(1, BX):
             acc = acc + v_ref[i, x] * applied[x]
+        diff_x = [v_ref[i, 0, :, :HZ] - hxlo[i, :, :HZ], v_ref[i, BX - 1, :, HZ:] - hxup[i, :, HZ:]]
+        diff_y = [pylo[i, :, :HZ] - hylo[i, :, :HZ], pyhi[i, :, HZ:] - hyup[i, :, HZ:]]
+        acc = acc + flow_x * jnp.concatenate(diff_x, axis=1)
+        acc = acc + flow_y * jnp.concatenate(diff_y, axis=1)
         proj_acc[i] = fold(acc)
     corr_col = jnp.sum(proj_acc[...].reshape(NV, HZ), axis=1, keepdims=True)
     line_at = lax.broadcasted_iota(jnp.int32, (1, 128), 1)
@@ -466,7 +571,9 @@
                 vm((NV, 128), F32),
                 vm(cell, F32),
             ]
-            + [vm((8, BZ), F32)] * 6
+            + [vm((8, BZ), F32)] * 2
+            + [vm((4, 8, 8, BZ), F32)]
+            + [vm((NV + 1, 8, BZ), F32)] * 4
             + [
                 vm((3, ROWS, 128), F32),
                 vm((3, 1, 128), F32),

time: 51.7 us -> 48.9 us (0.946)
  Pallas kernels: 50.3 us -> 47.4 us
    pallas_call x1, Pallas kernels: 50.3 us -> 47.4 us  [on_device(): pl.pallas_call(functools.partial(kernel, n_gx, n_gy), out_shape=[vm(cell,...]
where the time goes in v5:
time: 48.9 us; the launch traced here: 48.7 us
  Pallas kernels  47.4 us (97%)
  other arithmetic  0.66 us (1%)
  between operations  0.64 us (1%)
    pallas_call x1, Pallas kernels, on_device(): pl.pallas_call(functools.partial(kernel, n_gx, n_gy), out_shape=[vm(cell,...  47.4 us

profile of v5, /device:TPU:1, one launch (start us, length us, event | category | flops | bytes accessed | tf_op | source)
XLA Modules:
  0.0 48.7 jit_solution(5405568605592202406)
XLA Ops:
  0.6 47.4 %shard_map.59 = (f32[8,8,256]{2,1,0:T(8,128)S(1)}, f32[8,8,256]{2,1,0:T(8,128)S(1)}) custom-call(f32[32,8,8,256]{3,2,1,0:T(8,128)} %basis_hbm.1, f32[8,8,256]{2,1,0:T(8,128)} %rhs_hbm.1, f32[8,8,256]{2,1,0:T(8,128)} %extra_hbm.1, f32[3,8,8,256]{3,2,1,0:T(8,128)} %coeff_hbm.1), custom_call_target="tpu_custom_call" | custom-call | tf_op jit(solution)/shard_map/pallas_call | solution.py:552
  48.1 0.7 %fusion = (f32[8,8,256]{2,1,0:T(8,128)}, f32[8,8,256]{2,1,0:T(8,128)}) fusion(f32[8,8,256]{2,1,0:T(8,128)S(1)} %get-tuple-element.5, f32[8,8,256]{2,1,0:T(8,128)S(1)} %get-tuple-element.4), kind=kLoop, calls=%fused_computation.1 | loop fusion | flops 32768 | bytes 262144 | tf_op jit(solution)/shard_map/add | solution.py:597

commit v6 on v5

--- a/solution.py
+++ b/solution.py
@@ -76,10 +76,8 @@
     qy,
     src1,
     src2,
-    a1c,
     a1x,
     a1z,
-    a2c,
     a2x,
     a2z,
     load_sem,
@@ -106,8 +104,18 @@
     ]
     z_at = {t: (ix, (iy + n_gy + t) % n_gy) for t in (-4, -2, -1, 1, 2, 4)}
     core_peers = [(xy * 2 + (core + 1) % 2, iy)]
-    xy_peers = [(((xy + t) % n_xy) * 2 + core, iy) for t in range(1, n_xy)]
-    z_peers = [(ix, (iy + t) % n_gy) for t in range(1, n_gy)]
+    tall = n_xy // side
+
+    def steps(count):
+        return sorted(range(count), key=lambda t: -min(t, count - t))
+
+    hops = [(b, a, c) for b in range(tall) for a in range(side) for c in range(2) if a + b + c]
+    hops.sort(key=lambda t: -(min(t[0], tall - t[0]) + min(t[1], side - t[1])))
+    plane_peers = [
+        ((((y_at + b) % tall) * side + (x_at + a) % side) * 2 + (core + c) % 2, iy)
+        for b, a, c in hops
+    ]
+    z_peers = [(ix, (iy + t) % n_gy) for t in steps(n_gy) if t]
     first_x, last_x = ix == 0, ix == n_gx - 1
     first_y, last_y = iy == 0, iy == n_gy - 1
 
@@ -222,6 +230,7 @@
     pl.semaphore_wait(news.at[0], len(row_peers))
     pl.semaphore_wait(news.at[1], 2)
     tell([z_at[4], z_at[-4]], 2)
+    tell(core_peers, 3)
     prod[...] = dot_t(vh[...], ah[...]) + dot_t(vh[...], al[...]) + dot_t(vl[...], ah[...])
 
     for copy in x_first + y_first + c_sends:
@@ -386,8 +395,8 @@
         return jnp.sum(buf[...], axis=0)
 
     value = jnp.concatenate([packed, to_row(proj_col, 0)], axis=0)
-    value = stage(value, src1.at[0], a1c, 0, core, core_peers, 2)
-    value = stage(value, src1.at[1], a1x, 1, xy, xy_peers, n_xy)
+    pl.semaphore_wait(news.at[3], 1)
+    value = stage(value, src1.at[1], a1x, 1, ix, plane_peers, n_gx)
     pl.semaphore_wait(news.at[2], 2)
     value = stage(value, src1.at[2], a1z, 2, iy, z_peers, n_gy, boundary)
 
@@ -515,8 +524,7 @@
     value = to_row(corr_col, NV)
     value = jnp.where(line_at == 0, jnp.sum(fold(rd), axis=1, keepdims=True), value)
     value = jnp.where(line_at == 1, jnp.sum(fold(dad), axis=1, keepdims=True), value)
-    value = stage(value, src2.at[0], a2c, 3, core, core_peers, 2)
-    value = stage(value, src2.at[1], a2x, 4, xy, xy_peers, n_xy)
+    value = stage(value, src2.at[1], a2x, 4, ix, plane_peers, n_gx)
     value = stage(value, src2.at[2], a2z, 5, iy, z_peers, n_gy)
 
     shift = jnp.sum(inverse * value, axis=1, keepdims=True)
@@ -577,18 +585,16 @@
             + [
                 vm((3, ROWS, 128), F32),
                 vm((3, 1, 128), F32),
-                vm((2, ROWS, 128), F32),
-                vm((n_xy, ROWS, 128), F32),
+                vm((n_gx, ROWS, 128), F32),
                 vm((n_gy, ROWS, 128), F32),
-                vm((2, 1, 128), F32),
-                vm((n_xy, 1, 128), F32),
+                vm((n_gx, 1, 128), F32),
                 vm((n_gy, 1, 128), F32),
                 pltpu.SemaphoreType.DMA((CHUNKS + 3,)),
                 pltpu.SemaphoreType.DMA((14,)),
                 pltpu.SemaphoreType.DMA((14,)),
                 pltpu.SemaphoreType.DMA((6,)),
                 pltpu.SemaphoreType.DMA((6,)),
-                pltpu.SemaphoreType.REGULAR((3,)),
+                pltpu.SemaphoreType.REGULAR((4,)),
             ],
             compiler_params=pltpu.CompilerParams(
                 collective_id=0, has_side_effects=True, vmem_limit_bytes=63 << 20

time: 48.9 us -> 48.2 us (0.986)
  Pallas kernels: 47.4 us -> 46.7 us
    pallas_call x1, Pallas kernels: 47.4 us -> 46.7 us  [on_device(): pl.pallas_call(functools.partial(kernel, n_gx, n_gy), out_shape=[vm(cell,...]
where the time goes in v6:
time: 48.2 us; the launch traced here: 48.1 us
  Pallas kernels  46.7 us (97%)
  other arithmetic  0.66 us (1%)
  between operations  0.64 us (1%)
    pallas_call x1, Pallas kernels, on_device(): pl.pallas_call(functools.partial(kernel, n_gx, n_gy), out_shape=[vm(cell,...  46.7 us

profile of v6, /device:TPU:1, one launch (start us, length us, event | category | flops | bytes accessed | tf_op | source)
XLA Modules:
  0.0 48.1 jit_solution(11605628562825033438)
XLA Ops:
  0.6 46.7 %shard_map.59 = (f32[8,8,256]{2,1,0:T(8,128)S(1)}, f32[8,8,256]{2,1,0:T(8,128)S(1)}) custom-call(f32[32,8,8,256]{3,2,1,0:T(8,128)} %basis_hbm.1, f32[8,8,256]{2,1,0:T(8,128)} %rhs_hbm.1, f32[8,8,256]{2,1,0:T(8,128)} %extra_hbm.1, f32[3,8,8,256]{3,2,1,0:T(8,128)} %coeff_hbm.1), custom_call_target="tpu_custom_call" | custom-call | tf_op jit(solution)/shard_map/pallas_call | solution.py:560
  47.4 0.7 %fusion = (f32[8,8,256]{2,1,0:T(8,128)}, f32[8,8,256]{2,1,0:T(8,128)}) fusion(f32[8,8,256]{2,1,0:T(8,128)S(1)} %get-tuple-element.5, f32[8,8,256]{2,1,0:T(8,128)S(1)} %get-tuple-element.4), kind=kLoop, calls=%fused_computation.1 | loop fusion | flops 32768 | bytes 262144 | tf_op jit(solution)/shard_map/add | solution.py:603

commit v7 on v6

--- a/solution.py
+++ b/solution.py
@@ -86,6 +86,7 @@
     ar_send,
     ar_recv,
     news,
+    pick,
 ):
     ix = lax.axis_index("gx")
     iy = lax.axis_index("gy")
@@ -233,6 +234,21 @@
     tell(core_peers, 3)
     prod[...] = dot_t(vh[...], ah[...]) + dot_t(vh[...], al[...]) + dot_t(vl[...], ah[...])
 
+    s_row = lax.broadcasted_iota(jnp.int32, (4 * NV * BY, 128), 0)
+    s_col = lax.broadcasted_iota(jnp.int32, (4 * NV * BY, 128), 1)
+    pick[...] = (s_row // BY == s_col).astype(F32).astype(BF16)
+    eye_r = lax.broadcasted_iota(jnp.int32, (NV, 128), 0)
+    eye_l = lax.broadcasted_iota(jnp.int32, (NV, 128), 1)
+
+    def to_row(col, at):
+        return jnp.sum(jnp.where(eye_l == eye_r + at, col, 0.0), axis=0, keepdims=True)
+
+    def to_col(line, at):
+        return jnp.sum(jnp.where(eye_l == eye_r + at, line, 0.0), axis=1, keepdims=True)
+
+    proj_col = jnp.sum(proj_acc[...].reshape(NV, HZ), axis=1, keepdims=True)
+    proj_row = to_row(proj_col, 0)
+
     for copy in x_first + y_first + c_sends:
         copy.wait_recv()
     x_later = [
@@ -276,21 +292,12 @@
     total = jnp.where(same, total, 0.0)
     sums = jnp.sum(total.reshape(NV, BY, NV * BY), axis=1)
     wide = jnp.concatenate([sums[8 * k : 8 * k + 8] for k in range(4)], axis=1)
-    s_row = lax.broadcasted_iota(jnp.int32, (4 * NV * BY, 128), 0)
-    s_col = lax.broadcasted_iota(jnp.int32, (4 * NV * BY, 128), 1)
-    pick = (s_row // BY == s_col).astype(F32)
-    packed = jnp.dot(wide, pick, precision=lax.Precision.HIGHEST, preferred_element_type=F32)
-
-    eye_r = lax.broadcasted_iota(jnp.int32, (NV, 128), 0)
-    eye_l = lax.broadcasted_iota(jnp.int32, (NV, 128), 1)
-
-    def to_row(col, at):
-        return jnp.sum(jnp.where(eye_l == eye_r + at, col, 0.0), axis=0, keepdims=True)
-
-    def to_col(line, at):
-        return jnp.sum(jnp.where(eye_l == eye_r + at, line, 0.0), axis=1, keepdims=True)
-
-    proj_col = jnp.sum(proj_acc[...].reshape(NV, HZ), axis=1, keepdims=True)
+    first, second = split(wide)
+    third = (wide - first.astype(F32) - second.astype(F32)).astype(BF16)
+    packed = sum(
+        jnp.dot(part, pick[...], preferred_element_type=F32) for part in (third, second, first)
+    )
+
 
     def turned(v, low_edge, high_edge):
         return (
@@ -394,7 +401,7 @@
         ar_waits.append((others, at))
         return jnp.sum(buf[...], axis=0)
 
-    value = jnp.concatenate([packed, to_row(proj_col, 0)], axis=0)
+    value = jnp.concatenate([packed, proj_row], axis=0)
     pl.semaphore_wait(news.at[3], 1)
     value = stage(value, src1.at[1], a1x, 1, ix, plane_peers, n_gx)
     pl.semaphore_wait(news.at[2], 2)
@@ -495,8 +502,6 @@
         g_ref[x] = 0.5 * guess[x]
     dplo[...] = d_ref[:, 0, :]
     dphi[...] = d_ref[:, BY - 1, :]
-    w_row = to_row(weights, 0)
-    rest = proj - jnp.sum(gram * w_row, axis=1, keepdims=True)
 
     cells = [d_ref[x] for x in range(BX)]
     applied = apply_inside(cells)
@@ -524,7 +529,14 @@
     value = to_row(corr_col, NV)
     value = jnp.where(line_at == 0, jnp.sum(fold(rd), axis=1, keepdims=True), value)
     value = jnp.where(line_at == 1, jnp.sum(fold(dad), axis=1, keepdims=True), value)
-    value = stage(value, src2.at[1], a2x, 4, ix, plane_peers, n_gx)
+    kept = []
+
+    def solve_rest():
+        w_row = to_row(weights, 0)
+        kept.append(proj - jnp.sum(gram * w_row, axis=1, keepdims=True))
+
+    value = stage(value, src2.at[1], a2x, 4, ix, plane_peers, n_gx, solve_rest)
+    rest = kept[0]
     value = stage(value, src2.at[2], a2z, 5, iy, z_peers, n_gy)
 
     shift = jnp.sum(inverse * value, axis=1, keepdims=True)
@@ -595,6 +607,7 @@
                 pltpu.SemaphoreType.DMA((6,)),
                 pltpu.SemaphoreType.DMA((6,)),
                 pltpu.SemaphoreType.REGULAR((4,)),
+                vm((4 * NV * BY, 128), BF16),
             ],
             compiler_params=pltpu.CompilerParams(
                 collective_id=0, has_side_effects=True, vmem_limit_bytes=63 << 20

time: 48.2 us -> 48.1 us (level)
  no operation moved by 1% of the time
where the time goes in v7:
time: 48.1 us; the launch traced here: 47.9 us
  Pallas kernels  46.6 us (97%)
  other arithmetic  0.66 us (1%)
  between operations  0.64 us (1%)
    pallas_call x1, Pallas kernels, on_device(): pl.pallas_call(functools.partial(kernel, n_gx, n_gy), out_shape=[vm(cell,...  46.6 us

profile of v7, /device:TPU:1, one launch (start us, length us, event | category | flops | bytes accessed | tf_op | source)
XLA Modules:
  0.0 47.9 jit_solution(16486164072731312032)
XLA Ops:
  0.6 46.6 %shard_map.59 = (f32[8,8,256]{2,1,0:T(8,128)S(1)}, f32[8,8,256]{2,1,0:T(8,128)S(1)}) custom-call(f32[32,8,8,256]{3,2,1,0:T(8,128)} %basis_hbm.1, f32[8,8,256]{2,1,0:T(8,128)} %rhs_hbm.1, f32[8,8,256]{2,1,0:T(8,128)} %extra_hbm.1, f32[3,8,8,256]{3,2,1,0:T(8,128)} %coeff_hbm.1), custom_call_target="tpu_custom_call" | custom-call | tf_op jit(solution)/shard_map/pallas_call | solution.py:572
  47.2 0.7 %fusion = (f32[8,8,256]{2,1,0:T(8,128)}, f32[8,8,256]{2,1,0:T(8,128)}) fusion(f32[8,8,256]{2,1,0:T(8,128)S(1)} %get-tuple-element.5, f32[8,8,256]{2,1,0:T(8,128)S(1)} %get-tuple-element.4), kind=kLoop, calls=%fused_computation.1 | loop fusion | flops 32768 | bytes 262144 | tf_op jit(solution)/shard_map/add | solution.py:616
